TPU v7x, 256 devices: a whole 4x4x8 slice. The times are simulated.
256 devices in a mesh: mp: 8 (over z), fsdp: 32 (over y, x, core).
Axes of the slice: x: 4, y: 4, z: 8, core: 2. Of those that a mesh axis runs over, the one named last changes fastest.
Arguments:
- wide_momentum: float32 [2, 8192, 8192], P(None, 'mp', 'fsdp'), may hold values from -6 to 6
- wide_grad: bfloat16 [2, 8192, 8192], P(None, 'mp', 'fsdp'), may hold values from -6 to 6
- wide_basis: float32 [2, 8192, 256], P(None, 'fsdp'), may hold values from -0.0625 to 0.0625
- narrow_momentum: float32 [2, 1024, 8192], P(None, 'mp', 'fsdp'), may hold values from -6 to 6
- narrow_grad: bfloat16 [2, 1024, 8192], P(None, 'mp', 'fsdp'), may hold values from -6 to 6
- narrow_basis: float32 [2, 8192, 256], P(None, 'fsdp'), may hold values from -0.0625 to 0.0625
Outputs:
- wide_momentum_out: float32 [2, 8192, 8192], P(None, 'mp', 'fsdp')
- wide_basis_out: float32 [2, 8192, 256], P(None, 'fsdp')
- wide_update: bfloat16 [2, 8192, 8192], P(None, 'mp', 'fsdp')
- narrow_momentum_out: float32 [2, 1024, 8192], P(None, 'mp', 'fsdp')
- narrow_basis_out: float32 [2, 8192, 256], P(None, 'fsdp')
- narrow_update: bfloat16 [2, 1024, 8192], P(None, 'mp', 'fsdp')
All inputs are finite; a program needn't handle non-finite values.
Results may differ from a plain program's by a relative error of at most 0.0015.
Values sent between devices are 32-bit elements; how exact they have to be, the bound alone decides.
A program may use at most 64 MiB of HBM per device.

v0:
```python
import jax
import jax.numpy as jnp
from jax import lax
from jax.sharding import PartitionSpec as P

D = 8192
KVW = 1024
RANK = 256


EXACT_ARITHMETIC = lax.Precision.HIGHEST


def project(velocity_store, right_factor):
    return jnp.einsum("klc,kcq->klq", velocity_store, right_factor, precision=EXACT_ARITHMETIC)


def gram_of(mapped_lines):
    return jnp.einsum("xik,xih->xkh", mapped_lines, mapped_lines, precision=EXACT_ARITHMETIC)


def transpose_times(velocity_store, mapped_lines):
    return jnp.einsum("jms,jmu->jsu", velocity_store, mapped_lines, precision=EXACT_ARITHMETIC)


def right_inverse(lower, mapped_lines):
    solved = jax.vmap(lambda tri, rhs: jax.scipy.linalg.solve_triangular(tri, rhs, lower=True))(
        lower, jnp.swapaxes(mapped_lines, 1, 2)
    )
    return jnp.swapaxes(solved, 1, 2)


def complete_iteration(
    velocity_store, unit_basis_lines, triangular_root, inner_product_table, update_scale
):
    next_right_factor = triangular_root * lax.rsqrt(inner_product_table + 1e-06)[:, None, :]
    next_momentum = velocity_store - 0.05 * jnp.einsum(
        "ocd,old->ocl", unit_basis_lines, triangular_root, precision=EXACT_ARITHMETIC
    )
    weight_update = (
        update_scale
        * jnp.einsum(
            "ocd,old->ocl", unit_basis_lines, next_right_factor, precision=EXACT_ARITHMETIC
        )
    ).astype(jnp.bfloat16)
    return (next_momentum, next_right_factor, weight_update)


def local(wide_momentum, wide_grad, wide_basis, narrow_momentum, narrow_grad, narrow_basis):
    wide_buffer = wide_momentum + wide_grad.astype(jnp.float32)
    narrow_buffer = narrow_momentum + narrow_grad.astype(jnp.float32)
    wide_part = project(wide_buffer, wide_basis)
    narrow_part = project(narrow_buffer, narrow_basis)
    wide_rows, narrow_rows = lax.psum((wide_part, narrow_part), "fsdp")
    wide_gram = gram_of(wide_rows)
    narrow_gram = gram_of(narrow_rows)
    wide_total, narrow_total = lax.psum((wide_gram, narrow_gram), "mp")
    wide_ortho = right_inverse(jnp.linalg.cholesky(wide_total), wide_rows)
    narrow_ortho = right_inverse(jnp.linalg.cholesky(narrow_total), narrow_rows)
    wide_factor, narrow_factor = lax.psum(
        (transpose_times(wide_buffer, wide_ortho), transpose_times(narrow_buffer, narrow_ortho)),
        "mp",
    )
    wide_squares, narrow_squares = lax.psum(
        (
            jnp.sum(wide_factor * wide_factor, axis=1),
            jnp.sum(narrow_factor * narrow_factor, axis=1),
        ),
        "fsdp",
    )
    wide_scale = (D * D / RANK) ** 0.5
    narrow_scale = (KVW * D / RANK) ** 0.5
    wide_mom, wide_new, wide_upd = complete_iteration(
        wide_buffer, wide_ortho, wide_factor, wide_squares, wide_scale
    )
    narrow_mom, narrow_new, narrow_upd = complete_iteration(
        narrow_buffer, narrow_ortho, narrow_factor, narrow_squares, narrow_scale
    )
    return (wide_mom, wide_new, wide_upd, narrow_mom, narrow_new, narrow_upd)


def solution(mesh):
    return jax.shard_map(
        local,
        mesh=mesh,
        in_specs=(
            P(None, "mp", "fsdp"),
            P(None, "mp", "fsdp"),
            P(None, "fsdp", None),
            P(None, "mp", "fsdp"),
            P(None, "mp", "fsdp"),
            P(None, "fsdp", None),
        ),
        out_specs=(
            P(None, "mp", "fsdp"),
            P(None, "fsdp", None),
            P(None, "mp", "fsdp"),
            P(None, "mp", "fsdp"),
            P(None, "fsdp", None),
            P(None, "mp", "fsdp"),
        ),
        check_vma=False,
    )
```

profile of v0, /device:TPU:1, one launch (start us, length us, event | category | flops | bytes accessed | tf_op | source)
XLA Modules:
  0.0 630.6 jit_solution(9832630230841269322)
XLA Ops:
  8.2 5.2 fusion.5
  14.7 121.5 %all-reduce.9.cloned.1.call-done = (f32[2,1024,256]{2,1,0:T(8,128)}, f32[2,128,256]{2,1,0:T(8,128)}) async-done(((f32[2,1024,256]{2,1,0:T(8,128)}, f32[2,128,256]{2,1,0:T(8,128)}), (f32[2,1024,256]{2,1,0:T(8,128)}, f32[2,128,256]{2,1,0:T(8,128)})) %all-reduce.9.cloned.1.call-update) | async-done | bytes 2359312 | tf_op jit(solution)/shard_map/psum | solution.py:54
  136.2 6.6 %fusion.30 = f32[2,256,256]{1,2,0:T(8,128)} fusion(f32[2,1024,256]{2,1,0:T(8,128)} %get-tuple-element.45), kind=kOutput, calls=%fused_computation.78 | convolution fusion | flops 1610612736 | bytes 2621440 | tf_op jit(solution)/shard_map/xik,xih->xkh/dot_general | solution.py:19
  142.8 1.4 fusion.31
  146.3 70.0 %all-reduce.13.cloned.1.call-done = (f32[2,256,256]{1,2,0:T(8,128)}, f32[2,256,256]{1,2,0:T(8,128)}) async-done(((f32[2,256,256]{1,2,0:T(8,128)}, f32[2,256,256]{1,2,0:T(8,128)}), (f32[2,256,256]{1,2,0:T(8,128)}, f32[2,256,256]{1,2,0:T(8,128)})) %all-reduce.13.cloned.1.call-update) | async-done | bytes 1048592 | tf_op jit(solution)/shard_map/psum | solution.py:57
  216.2 1.3 copy.53
  219.8 23.5 %custom-call.26 = f32[2,128,128]{2,1,0:T(8,128)S(1)} custom-call(f32[2,128,128]{2,1,0:T(8,128)S(1)} %cholesky.201), custom_call_target="Cholesky" | custom-call | tf_op jit(solution)/shard_map/jit(cholesky)/cholesky | solution.py:59
  243.3 23.5 %custom-call.23 = f32[2,128,128]{2,1,0:T(8,128)S(1)} custom-call(f32[2,128,128]{2,1,0:T(8,128)S(1)} %cholesky.198), custom_call_target="Cholesky" | custom-call | tf_op jit(solution)/shard_map/jit(cholesky)/cholesky | solution.py:58
  267.6 19.7 %custom-call.27 = f32[2,1,128,128]{2,3,1,0:T(8,128)S(1)} custom-call(f32[2,1,128,128]{3,2,1,0:T(8,128)S(1)} %get-tuple-element.59), custom_call_target="InvertDiagBlocksLowerTriangular" | custom-call | tf_op jit(solution)/shard_map/jit(cholesky)/cholesky | solution.py:59
  289.7 23.7 %custom-call.28 = f32[2,128,128]{2,1,0:T(8,128)S(1)} custom-call(f32[2,128,128]{2,1,0:T(8,128)S(1)} %convolution_subtract_fusion.2), custom_call_target="Cholesky" | custom-call | tf_op jit(solution)/shard_map/jit(cholesky)/cholesky | solution.py:59
  313.5 19.7 %custom-call.24 = f32[2,1,128,128]{2,3,1,0:T(8,128)S(1)} custom-call(f32[2,1,128,128]{3,2,1,0:T(8,128)S(1)} %get-tuple-element.60), custom_call_target="InvertDiagBlocksLowerTriangular" | custom-call | tf_op jit(solution)/shard_map/jit(cholesky)/cholesky | solution.py:58
  333.8 23.5 %custom-call.25 = f32[2,128,128]{2,1,0:T(8,128)S(1)} custom-call(f32[2,128,128]{2,1,0:T(8,128)S(1)} %convolution_subtract_fusion.3), custom_call_target="Cholesky" | custom-call | tf_op jit(solution)/shard_map/jit(cholesky)/cholesky | solution.py:58
  358.8 4.0 while.2
  359.4 1.4 bitcast_dynamic-update-slice_fusion.4
  361.4 1.4 bitcast_dynamic-update-slice_fusion.4
  362.8 39.7 %custom-call.18 = f32[2,2,128,128]{2,3,1,0:T(8,128)S(1)} custom-call(f32[2,2,128,128]{3,2,1,0:T(8,128)S(1)} %bitcast.89), custom_call_target="InvertDiagBlocksLowerTriangular" | custom-call | tf_op jit(solution)/shard_map/vmap(jit(_solve_triangular))/triangular_solve | solution.py:27
  402.6 2.4 fusion.3
  405.0 3.2 convolution_subtract_fusion
  408.2 2.0 fusion.16
  410.2 4.4 fusion
  415.3 5.3 while.3
  415.9 2.1 bitcast_dynamic-update-slice_fusion.5
  418.6 2.1 bitcast_dynamic-update-slice_fusion.5
  420.6 40.9 %custom-call.19 = f32[2,2,128,128]{2,3,1,0:T(8,128)} custom-call(f32[2,2,128,128]{3,2,1,0:T(8,128)} %bitcast.88), custom_call_target="InvertDiagBlocksLowerTriangular" | custom-call | tf_op jit(solution)/shard_map/vmap(jit(_solve_triangular))/triangular_solve | solution.py:27
  463.2 1.3 fusion.10
  464.5 2.4 fusion.8
  467.0 74.7 %all-reduce.11.cloned.1.call-done = (f32[2,256,256]{2,1,0:T(8,128)}, f32[2,256,256]{2,1,0:T(8,128)}) async-done(((f32[2,256,256]{2,1,0:T(8,128)}, f32[2,256,256]{2,1,0:T(8,128)}), (f32[2,256,256]{2,1,0:T(8,128)}, f32[2,256,256]{2,1,0:T(8,128)})) %all-reduce.11.cloned.1.call-update) | async-done | bytes 1048592 | tf_op jit(solution)/shard_map/psum | solution.py:60
  541.7 6.9 %multiply_subtract_fusion = f32[2,1024,256]{2,1,0:T(8,128)} fusion(f32[2,256,256]{2,1,0:T(8,128)} %get-tuple-element.47, f32[2,128,1024]{2,1,0:T(8,128)S(1)} %fusion.16, f32[2,128,1024]{2,1,0:T(8,128)S(1)} %fusion.3, f32[2,1024,256]{2,1,0:T(8,128)} %param.7, bf16[2,1024,256]{2,1,0:T(8,128)(2,1)} %param.8), kind=kOutput, calls=%fused_computation.6 | convolution fusion | flops 1613234176 | bytes 7864320 | tf_op jit(solution)/shard_map/ocd,old->ocl/dot_general | solution.py:37
  548.7 1.4 fusion.1
  550.2 66.7 %all-reduce.1 = (f32[2,256]{1,0:T(2,128)S(1)}, f32[2,256]{1,0:T(2,128)S(1)}) all-reduce(f32[2,256]{1,0:T(2,128)S(1)} %multiply_reduce_fusion.1, f32[2,256]{1,0:T(2,128)S(1)} %multiply_reduce_fusion), channel_id=1, replica_groups=mesh['mp'=8,'fsdp'=32] {'fsdp'}, use_global_device_ids=true, to_apply=%region_8.10 | all-reduce | flops 1024 | bytes 8192 | tf_op jit(solution)/shard_map/psum | solution.py:64
  618.0 4.4 multiply_convert_fusion
  622.5 1.4 fusion.2
  (85 shorter events, 18.0 us)
Async XLA Ops:
  7.2 1.0 copy-start
  7.2 6.3 copy-start.15
  7.2 6.3 copy-start.6
  7.2 6.2 copy-start.13
  7.2 129.0 %all-reduce.9.cloned.1.call-start = ((), (), s32[]{:S(2)}) async-start(), calls=%async_computation | async-start | bytes 4718592 | tf_op jit(solution)/shard_map/psum | solution.py:54
  14.6 201.6 %all-reduce.13.cloned.1.call-start = ((), (), s32[]{:S(2)}) async-start(), calls=%async_computation.2 | async-start | bytes 2097152 | tf_op jit(solution)/shard_map/psum | solution.py:57
  136.2 6.6 %copy-start.5 = (f32[2,128,256]{2,1,0:T(8,128)S(1)}, f32[2,128,256]{2,1,0:T(8,128)}, u32[]{:S(2)}) copy-start(f32[2,128,256]{2,1,0:T(8,128)} %get-tuple-element.46) | copy-start | bytes 786436
  144.2 397.4 %all-reduce.11.cloned.1.call-start = ((), (), s32[]{:S(2)}) async-start(), calls=%async_computation.1 | async-start | bytes 2097152 | tf_op jit(solution)/shard_map/psum | solution.py:60
  216.2 2.6 copy-start.10
  216.2 2.6 copy-start.11
  219.0 0.8 copy-start.12
  266.8 91.1 %copy-start.17 = (pred[256,256]{1,0:T(8,128)(4,1)S(1)}, pred[256,256]{1,0:T(8,128)(4,1)}, u32[]{:S(2)}) copy-start(pred[256,256]{1,0:T(8,128)(4,1)} %iota_compare_fusion) | copy-start | bytes 196612
  402.6 2.4 copy-start.16
  405.0 5.2 copy-start.1
  405.0 5.2 copy-start.2
  541.7 6.9 %copy-start.4 = (f32[2,256,256]{2,1,0:T(8,128)S(1)}, f32[2,256,256]{2,1,0:T(8,128)}, u32[]{:S(2)}) copy-start(f32[2,256,256]{2,1,0:T(8,128)} %get-tuple-element.47) | copy-start | bytes 1572868
  541.7 7.0 %copy-start.3 = (f32[2,256,256]{2,1,0:T(8,128)S(1)}, f32[2,256,256]{2,1,0:T(8,128)}, u32[]{:S(2)}) copy-start(f32[2,256,256]{2,1,0:T(8,128)} %get-tuple-element.48) | copy-start | bytes 1572868
  541.7 7.1 %copy-start.7 = (f32[2,128,256]{2,1,0:T(8,128)S(1)}, f32[2,128,256]{2,1,0:T(8,128)}, u32[]{:S(2)}) copy-start(f32[2,128,256]{2,1,0:T(8,128)} %param.10) | copy-start | bytes 786436
  541.7 7.1 %copy-start.14 = (bf16[2,128,256]{2,1,0:T(8,128)(2,1)S(1)}, bf16[2,128,256]{2,1,0:T(8,128)(2,1)}, u32[]{:S(2)}) copy-start(bf16[2,128,256]{2,1,0:T(8,128)(2,1)} %param.11) | copy-start | bytes 393220
  618.0 4.5 copy-start.8
  622.5 1.4 copy-start.9
Sparse Core Ops, SparseCore 0:
  14.8 121.4 all-reduce.8
  144.4 71.8 all-reduce.12
  467.1 74.5 all-reduce.10
where the time goes:
time: 636 us; the launch traced here: 631 us
  waiting for transfers between devices  266 us (42%)
  other arithmetic  219 us (34%)
  blocking collectives  66.7 us (10%)
  matrix products  49 us (8%)
  local copies, waits for them, and re-layouts  15.2 us (2%)
  between operations  14.3 us (2%)
    psum x1, waiting for transfers between devices, local(): wide_rows, narrow_rows = lax.psum((wide_part, narrow_part), 'fsdp')  122 us
    another operation x5, other arithmetic, right_inverse(): jax.scipy.linalg.solve_triangular(tri, rhs, lower=True)  82 us
    psum x1, waiting for transfers between devices, local(): lax.psum((transpose_times(wide_buffer, wide_ortho), transpose_times(narro...  74.7 us
    psum x1, waiting for transfers between devices, local(): wide_total, narrow_total = lax.psum((wide_gram, narrow_gram), 'mp')  70 us
    another operation x8, other arithmetic, local(): narrow_ortho = right_inverse(jnp.linalg.cholesky(narrow_total), narrow_rows)  67.9 us
    another operation x8, other arithmetic, local(): wide_ortho = right_inverse(jnp.linalg.cholesky(wide_total), wide_rows)  67.5 us
    psum x1, blocking collectives, local(): lax.psum((jnp.sum(wide_factor * wide_factor, axis=1), jnp.sum(narrow_fact...  66.7 us
  transfers between devices with their start and end apart: 3, of which 3 were waited for; matrix products, arithmetic and copies ran while one was open for 0% of the time, Pallas kernels for 0%

commit v1 on v0

v1 whole, which is shorter than its diff:
```python
import functools

import jax
import jax.numpy as jnp
from jax import lax
from jax.experimental import pallas as pl
from jax.experimental.pallas import tpu as pltpu
from jax.sharding import PartitionSpec as P

D = 8192
KVW = 1024
RANK = 256
WIDE = 1024
NARROW = 128
COLS = 256
HALF = WIDE + NARROW
F32 = jnp.float32
BF16 = jnp.bfloat16
MESH = pl.DeviceIdType.MESH
EXACT = lax.Precision.HIGHEST

NN = (((1,), (0,)), ((), ()))
NT = (((1,), (1,)), ((), ()))
TN = (((0,), (0,)), ((), ()))


def exact_dot(a, b, dims=NN):
    return lax.dot_general(a, b, dims, precision=EXACT, preferred_element_type=F32)


def split(a):
    high = a.astype(BF16)
    return high, (a - high.astype(F32)).astype(BF16)


def bf16_dot(a, b, dims=NN):
    return lax.dot_general(a, b, dims, preferred_element_type=F32)


class Links:
    def __init__(self, send, recv):
        self.send, self.recv = send, recv
        self.count = 0
        self.started = []

    def start(self, src, dst, device):
        i = self.count
        self.count += 1
        copy = pltpu.make_async_remote_copy(
            src_ref=src,
            dst_ref=dst,
            send_sem=self.send.at[i],
            recv_sem=self.recv.at[i],
            device_id=device,
            device_id_type=MESH,
        )
        copy.start()
        self.started.append(copy)
        return copy

    def finish(self):
        for copy in self.started:
            copy.wait_send()


def ring_reduce(links, buf, out, h, base, chunk, cut, q, right, left, land):
    after, before = (q + 1) % 4, (q + 3) % 4

    def rows(c, lo, n):
        return pl.ds(pl.multiple_of(base + c * chunk + lo, 8), n)

    far = (q + 2) % 4
    a = links.start(buf.at[h, rows(far, 0, cut)], land.at[0, pl.ds(0, cut)], right)
    b = links.start(
        buf.at[h, rows(far, cut, chunk - cut)], land.at[1, pl.ds(0, chunk - cut)], left
    )
    yield
    a.wait_recv()
    buf[h, rows(after, 0, cut), :] += land[0, 0:cut, :]
    a = links.start(buf.at[h, rows(after, 0, chunk)], land.at[2, pl.ds(0, chunk)], right)
    b.wait_recv()
    buf[h, rows(before, cut, chunk - cut), :] += land[1, 0 : chunk - cut, :]
    b = links.start(buf.at[h, rows(before, 0, chunk)], land.at[3, pl.ds(0, chunk)], left)
    yield
    a.wait_recv()
    b.wait_recv()
    out[h, rows(q, 0, chunk), :] = (
        buf[h, rows(q, 0, chunk), :] + land[2, 0:chunk, :] + land[3, 0:chunk, :]
    )


def ring_gather(links, buf, h, base, chunk, cut, q, right, left):
    after, before = (q + 1) % 4, (q + 3) % 4

    def part(c, lo, n):
        return buf.at[h, pl.ds(pl.multiple_of(base + c * chunk + lo, 8), n)]

    own = part(q, 0, chunk)
    a = links.start(own, own, right)
    b = links.start(own, own, left)
    yield
    a.wait_recv()
    piece = part(before, 0, cut)
    a = links.start(piece, piece, right)
    b.wait_recv()
    piece = part(after, cut, chunk - cut)
    b = links.start(piece, piece, left)
    yield
    a.wait_recv()
    b.wait_recv()


def z_reduce_gather(links, buf, out, land, q, right, left):
    def chunk(ref, c):
        return ref.at[c % 8]

    def part(ref, c, lo):
        return ref.at[c % 8, pl.ds(lo, 64)]

    a = links.start(part(buf, q + 4, 0), land.at[0, 0, pl.ds(0, 64)], right)
    b = links.start(part(buf, q + 4, 64), land.at[1, 0, pl.ds(64, 64)], left)
    yield
    a.wait_recv()
    buf[(q + 3) % 8, 0:64, :] += land[0, 0, 0:64, :]
    a = links.start(chunk(buf, q + 3), land.at[0, 1], right)
    b.wait_recv()
    buf[(q + 5) % 8, 64:128, :] += land[1, 0, 64:128, :]
    b = links.start(chunk(buf, q + 5), land.at[1, 1], left)
    yield
    for s in (2, 3):
        a.wait_recv()
        buf[(q + 4 - s) % 8] += land[0, s - 1]
        a = links.start(chunk(buf, q + 4 - s), land.at[0, s], right)
        b.wait_recv()
        buf[(q + 4 + s) % 8] += land[1, s - 1]
        b = links.start(chunk(buf, q + 4 + s), land.at[1, s], left)
        yield
    a.wait_recv()
    b.wait_recv()
    out[q] = buf[q] + land[0, 3] + land[1, 3]
    a = links.start(chunk(out, q), chunk(out, q), right)
    b = links.start(chunk(out, q), chunk(out, q), left)
    yield
    for s in (1, 2):
        a.wait_recv()
        a = links.start(chunk(out, q + 8 - s), chunk(out, q + 8 - s), right)
        b.wait_recv()
        b = links.start(chunk(out, q + s), chunk(out, q + s), left)
        yield
    a.wait_recv()
    a = links.start(part(out, q + 5, 0), part(out, q + 5, 0), right)
    b.wait_recv()
    b = links.start(part(out, q + 3, 64), part(out, q + 3, 64), left)
    yield
    a.wait_recv()
    b.wait_recv()


def together(*stages):
    done = object()
    live = list(stages)
    while live:
        live = [s for s in live if next(s, done) is not done]


def block_inverse(e):
    lane = lax.broadcasted_iota(jnp.int32, (8, 128), 1)
    sub = lax.broadcasted_iota(jnp.int32, (8, 128), 0)
    group = (lane // 64) * 64

    def pick(tile, index):
        return jnp.take_along_axis(tile, group + index, axis=1)

    e = list(e)
    for g in range(4):
        cols = [[pick(e[i], 8 * g + t) for i in range(g, 4)] for t in range(8)]
        for t in range(8):
            inv = 1.0 / cols[t][0][t : t + 1, :]
            for n, i in enumerate(range(g, 4)):
                f = cols[t][n] * inv
                if n == 0:
                    f = jnp.where(sub > t, f, 0.0)
                e[i] = e[i] - f * e[g][t : t + 1, :]
                for s in range(t + 1, 8):
                    cols[s][n] = cols[s][n] - f * cols[s][0][t : t + 1, :]
    return [tile * lax.rsqrt(pick(tile, 8 * i + sub)) for i, tile in enumerate(e)]


def factor_block(a_ref, k):
    lane = lax.broadcasted_iota(jnp.int32, (32, 128), 1)
    row = lax.broadcasted_iota(jnp.int32, (32, 128), 0)
    eye = jnp.where(lane % 32 == row, 1.0, 0.0)
    d0 = a_ref[0, 0:32, 0:128]
    d1 = pltpu.roll(a_ref[1, 0:32, 0:128], 64, 1)
    e = jnp.where(
        lane < 32, d0, jnp.where((lane >= 64) & (lane < 96), d1, eye)
    )
    e = jnp.concatenate(block_inverse([e[8 * i : 8 * i + 8] for i in range(4)]), axis=0)
    col = lax.broadcasted_iota(jnp.int32, (32, 256), 1)
    wide_row = lax.broadcasted_iota(jnp.int32, (32, 256), 0)
    wide_eye = jnp.where(col == wide_row, 1.0, 0.0)
    for m in range(2):
        t = pltpu.roll(e, 96 - 64 * m, 1)[:, 0:32]
        panel = exact_dot(t, jnp.where(col < 32, wide_eye, a_ref[m, 0:32, :]))
        u = jnp.where((col >= 32) & (col < 256 - 32 * k), panel, 0.0)
        change = exact_dot(u, panel, TN)
        rest = lax.broadcasted_iota(jnp.int32, (224, 256), 1)
        rest = jnp.where(rest < 32, 0.0, a_ref[m, 32:256, :]) - change[32:256, :]
        a_ref[m, 0:224, :] = pltpu.roll(rest, 224, 1)
        a_ref[m, 224:256, :] = pltpu.roll(panel, 224, 1)


def main_kernel(
    wm, wg, wb, nm, ng, nb,
    ow, on, fac, sq,
    buf, part, full, swap, land_a, land_b, gram, slices, zland, gathered,
    wpart, wfull, wland, inverse, sq_a, sq_x, sq_y,
    send, recv,
):
    z = lax.axis_index("mp")
    f = lax.axis_index("fsdp")
    c = f % 2
    x = (f // 2) % 4
    y = f // 8

    def plane(xx, yy, cc):
        return {"fsdp": ((yy % 4) * 4 + xx % 4) * 2 + cc}

    sibling = plane(x, y, 1 - c)
    xs = [plane(x + d, y, c) for d in (1, 2, 3)]
    ys = [plane(x, y + d, c) for d in (1, 2, 3)]
    zs = [{"mp": (z + d) % 8} for d in range(1, 8)]

    barrier = pltpu.get_barrier_semaphore()
    partners = [sibling] + xs + ys + zs
    for device in partners:
        pl.semaphore_signal(barrier, inc=1, device_id=device, device_id_type=MESH)
    pl.semaphore_wait(barrier, len(partners))

    links = Links(send, recv)

    def raw_half(cc):
        base = cc * HALF

        def tile(r, n, moment, grad, basis):
            b = moment + grad.astype(F32)
            rows = pl.ds(pl.multiple_of(base + r, 8), n)
            buf[rows, :] = b
            raw = exact_dot(b, basis)
            part[0, rows, :] = raw[:, 0:128]
            part[1, rows, :] = raw[:, 128:256]

        @pl.loop(0, WIDE // 256)
        def _(i):
            rows = pl.ds(pl.multiple_of(i * 256, 256), 256)
            tile(i * 256, 256, wm[cc, rows, :], wg[cc, rows, :], wb[cc])

        tile(WIDE, NARROW, nm[cc], ng[cc], nb[cc])

    raw_half(1 - c)
    other = pl.ds(pl.multiple_of((1 - c) * HALF, 8), HALF)
    mine = pl.ds(pl.multiple_of(c * HALF, 8), HALF)
    exchange = links.start(part.at[:, other], swap, sibling)
    raw_half(c)
    exchange.wait_recv()
    part[:, mine, :] += swap[...]

    x_ring = dict(q=x, right=xs[0], left=xs[2])
    y_ring = dict(q=y, right=ys[0], left=ys[2])
    base = c * HALF
    big, small = HALF // 4, HALF // 16

    def reduce_both(h, first, second, land):
        yield from ring_reduce(
            links, part, part, h, base, big, 144, land=land.at[0], **first
        )
        yield from ring_reduce(
            links, part, full, h, base + first["q"] * big, small, 40, land=land.at[1], **second
        )

    def gather_both(buffer, h, start, sizes, cuts, first, second):
        yield from ring_gather(
            links, buffer, h, start + first["q"] * sizes[0], sizes[1], cuts[1], **second
        )
        yield from ring_gather(links, buffer, h, start, sizes[0], cuts[0], **first)

    together(reduce_both(0, x_ring, y_ring, land_a), reduce_both(1, y_ring, x_ring, land_b))
    together(
        gather_both(full, 0, base, (big, small), (144, 40), x_ring, y_ring),
        gather_both(full, 1, base, (big, small), (144, 40), y_ring, x_ring),
    )
    exchange = links.start(full.at[:, mine], full.at[:, mine], sibling)

    def raw_rows(start, n):
        rows = pl.ds(pl.multiple_of(start, 8), n)
        return jnp.concatenate([full[0, rows, :], full[1, rows, :]], axis=1)

    for kind, (start, n) in enumerate(((0, WIDE), (WIDE, NARROW))):
        raw = raw_rows(base + start, n)
        gram[kind] = exact_dot(raw, raw, TN)
    places = (x * 4 + y, y * 4 + x)
    for t in range(8):
        h, m, r = t // 4, (t // 2) % 2, t % 2
        rows = pl.ds(pl.multiple_of(places[h] * 16 + r * 8, 8), 8)
        slices[t] = gram[m, rows, h * 128 : h * 128 + 128]
    gram_sends = [
        links.start(slices.at[(z + d) % 8], zland.at[d - 1], zs[d - 1]) for d in range(1, 8)
    ]

    exchange.wait_recv()
    for m in range(4):
        start, n = ((0, WIDE), (HALF, WIDE), (WIDE, NARROW), (HALF + WIDE, NARROW))[m]
        w = exact_dot(buf[start : start + n, :], raw_rows(start, n), TN)
        for k in range(8):
            wpart[k, m * 32 : m * 32 + 32, :] = w[k * 32 : k * 32 + 32, :]
    w_sum = z_reduce_gather(links, wpart, wfull, wland, z, zs[0], zs[6])
    next(w_sum)

    for copy in gram_sends:
        copy.wait_recv()
    total = slices[z]
    for d in range(7):
        total = total + zland[d]
    place = places[0] + (z // 4) * (places[1] - places[0])
    own = gathered.at[z // 4, pl.ds(pl.multiple_of(place * 32 + (z % 4) * 8, 8), 8)]
    own[...] = total
    gram_sends = [links.start(own, own, zs[d]) for d in range(7)]
    next(w_sum)
    for copy in gram_sends:
        copy.wait_recv()
    together(
        gather_both(gathered, 0, 0, (128, 32), (64, 16), x_ring, y_ring),
        gather_both(gathered, 1, 0, (128, 32), (64, 16), y_ring, x_ring),
    )
    for h in range(2):
        for p in range(16):
            for m in range(2):
                gram[m, p * 16 : p * 16 + 16, h * 128 : h * 128 + 128] = gathered[
                    h, p * 32 + m * 16 : p * 32 + m * 16 + 16, :
                ]

    for k in range(0, 8, 2):
        lax.fori_loop(k, k + 2, lambda i, _: factor_block(gram, i), None)
        next(w_sum, None)
    inverse[c] = gram[...]
    exchange = links.start(inverse.at[c], inverse.at[c], sibling)
    for _ in w_sum:
        pass
    exchange.wait_recv()

    for m in range(4):
        w = jnp.concatenate([wfull[k, m * 32 : m * 32 + 32, :] for k in range(8)], axis=0)
        factor = exact_dot(w, inverse[m % 2, m // 2], NT)
        fac[m] = factor
        squares = jnp.sum(factor * factor, axis=0, keepdims=True)
        for h in range(2):
            row = 2 * m + h
            sq[row : row + 1, :] = squares[:, h * 128 : h * 128 + 128]
    sq_a[0] = sq[...]
    exchange = links.start(sq_a.at[0], sq_a.at[1], sibling)

    def ortho_half(cc):
        start = cc * HALF
        for m, (lo, n) in enumerate(((0, WIDE), (WIDE, NARROW))):
            o = exact_dot(raw_rows(start + lo, n), inverse[cc, m], NT)
            if m == 0:
                ow[cc] = o
            else:
                on[cc] = o

    exchange.wait_recv()
    sq_x[0] = sq_a[0] + sq_a[1]
    sends = [links.start(sq_x.at[0], sq_x.at[d + 1], xs[d]) for d in range(3)]
    ortho_half(0)
    for copy in sends:
        copy.wait_recv()
    sq_y[0] = sq_x[0] + sq_x[1] + sq_x[2] + sq_x[3]
    sends = [links.start(sq_y.at[0], sq_y.at[d + 1], ys[d]) for d in range(3)]
    ortho_half(1)
    for copy in sends:
        copy.wait_recv()
    sq[...] = sq_y[0] + sq_y[1] + sq_y[2] + sq_y[3]
    links.finish()


def last_kernel(wm, wg, nm, ng, ow, on, fac, sq, wmo, wbo, wup, nmo, nbo, nup):
    for kind, (moment, grad, ortho, m_out, b_out, update, rows) in enumerate(
        ((wm, wg, ow, wmo, wbo, wup, D), (nm, ng, on, nmo, nbo, nup, KVW))
    ):
        factor = fac[kind, 0]
        basis = factor * lax.rsqrt(sq[kind, 0] + 1e-6)
        b_out[0] = basis
        o_high, o_low = split(ortho[0])
        b_high, b_low = split(basis)
        m_out[0] = (
            moment[0]
            + grad[0].astype(F32)
            - 0.05 * bf16_dot(o_high, factor.astype(BF16), NT)
        )
        product = bf16_dot(o_high, b_high, NT) + (
            bf16_dot(o_high, b_low, NT) + bf16_dot(o_low, b_high, NT)
        )
        update[0] = ((rows * D / RANK) ** 0.5 * product).astype(BF16)


def local(wide_momentum, wide_grad, wide_basis, narrow_momentum, narrow_grad, narrow_basis):
    vmem = pl.BlockSpec(memory_space=pltpu.VMEM)
    copies = 128
    ow, on, fac, sq = pl.pallas_call(
        main_kernel,
        out_shape=(
            jax.ShapeDtypeStruct((2, WIDE, RANK), F32),
            jax.ShapeDtypeStruct((2, NARROW, RANK), F32),
            jax.ShapeDtypeStruct((4, COLS, RANK), F32),
            jax.ShapeDtypeStruct((8, 128), F32),
        ),
        in_specs=[vmem] * 6,
        out_specs=[vmem] * 4,
        scratch_shapes=[
            pltpu.VMEM((2 * HALF, COLS), F32),
            pltpu.VMEM((2, 2 * HALF, 128), F32),
            pltpu.VMEM((2, 2 * HALF, 128), F32),
            pltpu.VMEM((2, HALF, 128), F32),
            pltpu.VMEM((2, 4, HALF // 4, 128), F32),
            pltpu.VMEM((2, 4, HALF // 4, 128), F32),
            pltpu.VMEM((2, RANK, RANK), F32),
            pltpu.VMEM((8, 8, 128), F32),
            pltpu.VMEM((7, 8, 128), F32),
            pltpu.VMEM((2, 512, 128), F32),
            pltpu.VMEM((8, 128, RANK), F32),
            pltpu.VMEM((8, 128, RANK), F32),
            pltpu.VMEM((2, 4, 128, RANK), F32),
            pltpu.VMEM((2, 2, RANK, RANK), F32),
            pltpu.VMEM((2, 8, 128), F32),
            pltpu.VMEM((4, 8, 128), F32),
            pltpu.VMEM((4, 8, 128), F32),
            pltpu.SemaphoreType.DMA((copies,)),
            pltpu.SemaphoreType.DMA((copies,)),
        ],
        compiler_params=pltpu.CompilerParams(
            collective_id=0, has_side_effects=True, vmem_limit_bytes=48 * 2**20
        ),
    )(wide_momentum, wide_grad, wide_basis, narrow_momentum, narrow_grad, narrow_basis)

    def rows(n):
        return pl.BlockSpec((1, n, COLS), lambda m, i: (m, i, 0))

    def whole(*lead):
        return pl.BlockSpec(lead, lambda m, i: (0, m, 0, 0))

    basis_out = pl.BlockSpec((1, COLS, RANK), lambda m, i: (m, 0, 0))
    steps = 4
    w, n = WIDE // steps, NARROW // steps
    return pl.pallas_call(
        last_kernel,
        grid=(2, steps),
        out_shape=(
            jax.ShapeDtypeStruct((2, WIDE, COLS), F32),
            jax.ShapeDtypeStruct((2, COLS, RANK), F32),
            jax.ShapeDtypeStruct((2, WIDE, COLS), BF16),
            jax.ShapeDtypeStruct((2, NARROW, COLS), F32),
            jax.ShapeDtypeStruct((2, COLS, RANK), F32),
            jax.ShapeDtypeStruct((2, NARROW, COLS), BF16),
        ),
        in_specs=[
            rows(w), rows(w), rows(n), rows(n), rows(w), rows(n),
            whole(2, 1, COLS, RANK), whole(2, 1, 1, RANK),
        ],
        out_specs=[rows(w), basis_out, rows(w), rows(n), basis_out, rows(n)],
        compiler_params=pltpu.CompilerParams(vmem_limit_bytes=32 * 2**20),
    )(
        wide_momentum, wide_grad, narrow_momentum, narrow_grad, ow, on,
        fac.reshape(2, 2, COLS, RANK), sq.reshape(2, 2, 1, RANK),
    )


def solution(mesh):
    return jax.shard_map(
        local,
        mesh=mesh,
        in_specs=(
            P(None, "mp", "fsdp"),
            P(None, "mp", "fsdp"),
            P(None, "fsdp", None),
            P(None, "mp", "fsdp"),
            P(None, "mp", "fsdp"),
            P(None, "fsdp", None),
        ),
        out_specs=(
            P(None, "mp", "fsdp"),
            P(None, "fsdp", None),
            P(None, "mp", "fsdp"),
            P(None, "mp", "fsdp"),
            P(None, "fsdp", None),
            P(None, "mp", "fsdp"),
        ),
        check_vma=False,
    )
```

time: 636 us -> 127 us (0.20)
  waiting for transfers between devices: 266 us -> 0 us
  other arithmetic: 219 us -> 0 us
  Pallas kernels: 0 us -> 121 us
  blocking collectives: 66.7 us -> 0 us
  matrix products: 49 us -> 0 us
  between operations: 14.3 us -> 0.7 us
  local copies, waits for them, and re-layouts: 15.2 us -> 5.31 us
    psum x3 -> x0, waiting for transfers between devices: 266 us -> none  [the longest x1 122 us: local(): wide_rows, narrow_rows = lax.psum((wide_part, narrow_part), 'fsdp')]
    another operation x21 -> x0, other arithmetic: 217 us -> none  [the longest x5 82 us: right_inverse(): jax.scipy.linalg.solve_triangular(tri, rhs, lower=True)]
    pallas_call x0 -> x2, Pallas kernels: none -> 121 us  [the longest x1 116 us: local(): pl.pallas_call(main_kernel, out_shape=(jax.ShapeDtypeStruct((2, WIDE, RAN...]
    psum x1 -> x0, blocking collectives: 66.7 us -> none  [local(): lax.psum((jnp.sum(wide_factor * wide_factor, axis=1), jnp.sum(narrow_fact...]
    dot_general x10 -> x0, matrix products: 35.3 us -> none  [the longest x2 8.37 us: complete_iteration(): jnp.einsum('ocd,old->ocl', unit_basis_lines, triangular_root, precision=E...]
    another operation x10 -> x0, matrix products: 13.7 us -> none  [the longest x6 10.5 us: right_inverse(): jax.scipy.linalg.solve_triangular(tri, rhs, lower=True)]
    another operation x17 -> x0, local copies, waits for them, and re-layouts: 10.1 us -> none
  transfers between devices with their start and end apart: 3 -> 0, of which waited for: 3 -> 0; matrix products, arithmetic and copies ran while one was open for 0% -> 0% of each run, Pallas kernels for 0% -> 0%
where the time goes in v1:
time: 127 us
  Pallas kernels  121 us (95%)
  local copies, waits for them, and re-layouts  5.31 us (4%)
    pallas_call x1, Pallas kernels, local(): pl.pallas_call(main_kernel, out_shape=(jax.ShapeDtypeStruct((2, WIDE, RAN...  116 us
    unnamed x12, local copies, waits for them, and re-layouts  5.31 us
    pallas_call x1, Pallas kernels, local(): pl.pallas_call(last_kernel, grid=(2, steps), out_shape=(jax.ShapeDtypeStr...  5.3 us

profile of v1, /device:TPU:1, one launch (start us, length us, event | category | flops | bytes accessed | tf_op | source)
XLA Modules:
  0.0 127.0 jit_solution(12129044148161786080)
XLA Ops:
  0.6 0.0 copy-start
  0.6 0.0 copy-start.1
  0.7 1.4 %copy-done.1 = bf16[2,1024,256]{2,1,0:T(8,128)(2,1)S(1)} copy-done((bf16[2,1024,256]{2,1,0:T(8,128)(2,1)S(1)}, bf16[2,1024,256]{2,1,0:T(8,128)(2,1)}, u32[]{:S(2)}) %copy-start.1) | copy-done | bytes 1048600
  2.0 0.0 copy-start.2
  2.0 0.9 copy-done.2
  3.0 0.0 copy-start.3
  3.0 1.0 copy-done.3
  4.0 0.0 copy-start.4
  4.0 1.0 copy-done.4
  5.1 0.0 copy-start.5
  5.1 0.9 copy-done.5
  6.0 115.7 %shard_map.109 = (f32[2,1024,256]{2,1,0:T(8,128)S(1)}, f32[2,128,256]{2,1,0:T(8,128)S(1)}, f32[4,256,256]{2,1,0:T(8,128)S(1)}, f32[8,128]{1,0:T(8,128)S(1)}) custom-call(f32[2,1024,256]{2,1,0:T(8,128)} %wm.3, bf16[2,1024,256]{2,1,0:T(8,128)(2,1)S(1)} %copy-done.1, f32[2,256,256]{2,1,0:T(8,128)S(1)} %copy-done.3, f32[2,128,256]{2,1,0:T(8,128)S(1)} %copy-done.2, ...), custom_call_target="tpu_custom_call" | custom-call | tf_op jit(solution)/shard_map/pallas_call | solution.py:409
  121.7 0.0 copy-done
  121.7 5.3 %shard_map.110 = (f32[2,1024,256]{2,1,0:T(8,128)}, f32[2,256,256]{2,1,0:T(8,128)}, bf16[2,1024,256]{2,1,0:T(8,128)(2,1)}, f32[2,128,256]{2,1,0:T(8,128)}, f32[2,...) custom-call(f32[2,1024,256]{2,1,0:T(8,128)S(1)} %copy-done, bf16[2,1024,256]{2,1,0:T(8,128)(2,1)S(1)} %copy-done.1, ...), custom_call_target="tpu_custom_call" | custom-call | tf_op jit(solution)/shard_map/pallas_call | solution.py:454
Async XLA Ops:
  0.6 121.0 %copy-start = (f32[2,1024,256]{2,1,0:T(8,128)S(1)}, f32[2,1024,256]{2,1,0:T(8,128)}, u32[]{:S(2)}) copy-start(f32[2,1024,256]{2,1,0:T(8,128)} %wm.3) | copy-start | bytes 6291460
  0.6 1.4 %copy-start.1 = (bf16[2,1024,256]{2,1,0:T(8,128)(2,1)S(1)}, bf16[2,1024,256]{2,1,0:T(8,128)(2,1)}, u32[]{:S(2)}) copy-start(bf16[2,1024,256]{2,1,0:T(8,128)(2,1)} %wg.3) | copy-start | bytes 3145732
  2.0 0.9 copy-start.2
  3.0 1.0 copy-start.3
  4.0 1.0 copy-start.4
  5.1 0.9 copy-start.5

commit v2 on v1

v2 whole, which is shorter than its diff:
```python
import jax
import jax.numpy as jnp
from jax import lax
from jax.experimental import pallas as pl
from jax.experimental.pallas import tpu as pltpu
from jax.sharding import PartitionSpec as P

D = 8192
KVW = 1024
RANK = 256
WIDE = 1024
NARROW = 128
COLS = 256
HALF = WIDE + NARROW
F32 = jnp.float32
BF16 = jnp.bfloat16
MESH = pl.DeviceIdType.MESH
EXACT = lax.Precision.HIGHEST

NN = (((1,), (0,)), ((), ()))
NT = (((1,), (1,)), ((), ()))
TN = (((0,), (0,)), ((), ()))


def exact_dot(a, b, dims=NN):
    return lax.dot_general(a, b, dims, precision=EXACT, preferred_element_type=F32)


def split(a):
    high = a.astype(BF16)
    return high, (a - high.astype(F32)).astype(BF16)


def bf16_dot(a, b, dims=NN):
    return lax.dot_general(a, b, dims, preferred_element_type=F32)


class Links:
    def __init__(self, send, recv):
        self.send, self.recv = send, recv
        self.count = 0
        self.started = []

    def start(self, src, dst, device):
        i = self.count
        self.count += 1
        copy = pltpu.make_async_remote_copy(
            src_ref=src,
            dst_ref=dst,
            send_sem=self.send.at[i],
            recv_sem=self.recv.at[i],
            device_id=device,
            device_id_type=MESH,
        )
        copy.start()
        self.started.append(copy)
        return copy

    def finish(self):
        for copy in self.started:
            copy.wait_send()


def ring_reduce(links, buf, out, h, base, chunk, cut, q, right, left, land):
    after, before = (q + 1) % 4, (q + 3) % 4

    def rows(c, lo, n):
        return pl.ds(pl.multiple_of(base + c * chunk + lo, 8), n)

    far = (q + 2) % 4
    a = links.start(buf.at[h, rows(far, 0, cut)], land.at[0, pl.ds(0, cut)], right)
    b = links.start(
        buf.at[h, rows(far, cut, chunk - cut)], land.at[1, pl.ds(0, chunk - cut)], left
    )
    yield
    a.wait_recv()
    buf[h, rows(after, 0, cut), :] += land[0, 0:cut, :]
    a = links.start(buf.at[h, rows(after, 0, chunk)], land.at[2, pl.ds(0, chunk)], right)
    b.wait_recv()
    buf[h, rows(before, cut, chunk - cut), :] += land[1, 0 : chunk - cut, :]
    b = links.start(buf.at[h, rows(before, 0, chunk)], land.at[3, pl.ds(0, chunk)], left)
    yield
    a.wait_recv()
    b.wait_recv()
    out[h, rows(q, 0, chunk), :] = (
        buf[h, rows(q, 0, chunk), :] + land[2, 0:chunk, :] + land[3, 0:chunk, :]
    )


def ring_gather(links, buf, h, base, chunk, cut, q, right, left):
    after, before = (q + 1) % 4, (q + 3) % 4

    def part(c, lo, n):
        return buf.at[h, pl.ds(pl.multiple_of(base + c * chunk + lo, 8), n)]

    own = part(q, 0, chunk)
    a = links.start(own, own, right)
    b = links.start(own, own, left)
    yield
    a.wait_recv()
    piece = part(before, 0, cut)
    a = links.start(piece, piece, right)
    b.wait_recv()
    piece = part(after, cut, chunk - cut)
    b = links.start(piece, piece, left)
    yield
    a.wait_recv()
    b.wait_recv()


def z_reduce_gather(links, buf, out, land, lo, n, q, right, left):
    half = n // 2

    def part(ref, i, start, size):
        return ref.at[i, pl.ds(lo + start, size)]

    def chunk(ref, i):
        return part(ref, i % 8, 0, n)

    def add(i, slot, start, size):
        rows = slice(lo + start, lo + start + size)
        buf[i % 8, rows, :] += land[slot[0], slot[1], rows, :]

    a = links.start(
        part(buf, (q + 4) % 8, 0, half), part(land.at[0], 0, 0, half), right
    )
    b = links.start(
        part(buf, (q + 4) % 8, half, half), part(land.at[1], 0, half, half), left
    )
    yield
    for s in (1, 2, 3):
        size = half if s == 1 else n
        a.wait_recv()
        add(q + 4 - s, (0, s - 1), 0, size)
        a = links.start(chunk(buf, q + 4 - s), part(land.at[0], s, 0, n), right)
        b.wait_recv()
        add(q + 4 + s, (1, s - 1), n - size, size)
        b = links.start(chunk(buf, q + 4 + s), part(land.at[1], s, 0, n), left)
        yield
    a.wait_recv()
    b.wait_recv()
    rows = slice(lo, lo + n)
    out[q, rows, :] = buf[q, rows, :] + land[0, 3, rows, :] + land[1, 3, rows, :]
    a = links.start(chunk(out, q), chunk(out, q), right)
    b = links.start(chunk(out, q), chunk(out, q), left)
    yield
    for s in (1, 2):
        a.wait_recv()
        a = links.start(chunk(out, q + 8 - s), chunk(out, q + 8 - s), right)
        b.wait_recv()
        b = links.start(chunk(out, q + s), chunk(out, q + s), left)
        yield
    a.wait_recv()
    piece = part(out, (q + 5) % 8, 0, half)
    a = links.start(piece, piece, right)
    b.wait_recv()
    piece = part(out, (q + 3) % 8, half, half)
    b = links.start(piece, piece, left)
    yield
    a.wait_recv()
    b.wait_recv()


def together(*stages):
    done = object()
    live = list(stages)
    while live:
        live = [s for s in live if next(s, done) is not done]


def block_inverse(e):
    lane = lax.broadcasted_iota(jnp.int32, (8, 128), 1)
    sub = lax.broadcasted_iota(jnp.int32, (8, 128), 0)
    group = (lane // 64) * 64

    def pick(tile, index):
        return jnp.take_along_axis(tile, group + index, axis=1)

    e = list(e)
    for g in range(4):
        cols = [[pick(e[i], 8 * g + t) for i in range(g, 4)] for t in range(8)]
        for t in range(8):
            pivot = cols[t][0][t : t + 1, :]
            inv = pl.reciprocal(pivot, approx=True)
            inv = inv * (2.0 - pivot * inv)
            for n, i in enumerate(range(g, 4)):
                f = cols[t][n] * inv
                if n == 0:
                    f = jnp.where(sub > t, f, 0.0)
                e[i] = e[i] - f * e[g][t : t + 1, :]
                for s in range(t + 1, 8):
                    cols[s][n] = cols[s][n] - f * cols[s][0][t : t + 1, :]
    return [tile * lax.rsqrt(pick(tile, 8 * i + sub)) for i, tile in enumerate(e)]


def factor_block(a_ref, k):
    at = 32 * k
    base = at // 128 * 128
    off = at - base
    lane = lax.broadcasted_iota(jnp.int32, (32, 128), 1)
    row = lax.broadcasted_iota(jnp.int32, (32, 128), 0)
    eye = jnp.where(lane % 32 == row, 1.0, 0.0)

    def turned(v, by):
        return pltpu.roll(v, by % 128, 1) if by % 128 else v

    d0, d1 = (a_ref[m, at : at + 32, base : base + 128] for m in range(2))
    d0, d1 = turned(d0, -off), turned(d1, 64 - off)
    e = jnp.where(lane < 32, d0, jnp.where((lane >= 64) & (lane < 96), d1, eye))
    e = jnp.concatenate(block_inverse([e[8 * i : 8 * i + 8] for i in range(4)]), axis=0)
    col = lax.broadcasted_iota(jnp.int32, (32, 256), 1)
    wide_row = lax.broadcasted_iota(jnp.int32, (32, 256), 0)
    inside = (col >= at) & (col < at + 32)
    wide_eye = jnp.where(col - at == wide_row, 1.0, 0.0)
    below = at + 32
    low = below // 128 * 128
    for m in range(2):
        t = turned(e, 96 - 64 * m)[:, 0:32]
        panel = exact_dot(t, jnp.where(inside, wide_eye, a_ref[m, at : at + 32, :]))
        a_ref[m, at : at + 32, :] = panel
        if below < 256:
            change = exact_dot(panel[:, low:256], panel, TN)
            under = lax.broadcasted_iota(jnp.int32, (256 - below, 256), 1)
            rest = jnp.where(
                (under >= at) & (under < below), 0.0, a_ref[m, below:256, :]
            )
            a_ref[m, below:256, :] = rest - change[below - low :, :]


def main_kernel(
    wm_in, wg_in, wb_in, nm_in, ng_in, nb_in,
    ow_out, on_out, fac_out, sq_out,
    ow, on, fac, sq,
    wm, wg, wb, nm, ng, nb,
    bh, bl, vh, vl, part, full, swap, land, gram, slices, zland, gathered,
    wpart, wfull, wland, inverse, sq_x, sq_y,
    load, store, send, recv,
):
    z = lax.axis_index("mp")
    f = lax.axis_index("fsdp")
    c = f % 2
    x = (f // 2) % 4
    y = f // 8

    loads = []
    for i, cc in enumerate((1 - c, c)):
        pairs = ((wb_in, wb), (wg_in, wg), (wm_in, wm), (nb_in, nb), (ng_in, ng), (nm_in, nm))
        for n, (src, dst) in enumerate(pairs):
            copy = pltpu.make_async_copy(src.at[cc], dst.at[cc], load.at[6 * i + n])
            copy.start()
            loads.append(copy)

    def plane(xx, yy, cc):
        return {"fsdp": ((yy % 4) * 4 + xx % 4) * 2 + cc}

    sibling = plane(x, y, 1 - c)
    xs = [plane(x + d, y, c) for d in (1, 2, 3)]
    xos = [plane(x + d, y, 1 - c) for d in (1, 2, 3)]
    ys = [plane(x, y + d, c) for d in (1, 2, 3)]
    zs = [{"mp": (z + d) % 8} for d in range(1, 8)]

    barrier = pltpu.get_barrier_semaphore()
    partners = [sibling] + xs + xos + ys + zs
    for device in partners:
        pl.semaphore_signal(barrier, inc=1, device_id=device, device_id_type=MESH)

    links = Links(send, recv)
    sets = ((0, 640), (640, 512))
    wide_b = WIDE - 640

    def split_basis(cc):
        for kind, basis in enumerate((wb, nb)):
            high, low = split(basis[cc])
            vh[cc, kind] = high
            vl[cc, kind] = low

    def raw_rows_of(cc, kind, r, n, moment, grad):
        rows = pl.ds(pl.multiple_of(cc * HALF + r, 16), n)
        high, low = split(moment + grad.astype(F32))
        bh[rows, :] = high
        bl[rows, :] = low
        v_high = vh[cc, kind]
        raw = bf16_dot(high, v_high) + (bf16_dot(high, vl[cc, kind]) + bf16_dot(low, v_high))
        part[0, rows, :] = raw[:, 0:128]
        part[1, rows, :] = raw[:, 128:256]

    def raw_set(cc, i):
        lo, n = ((0, 640), (640, wide_b))[i]
        step = 128

        @pl.loop(0, n // step)
        def _(j):
            rows = pl.ds(pl.multiple_of(lo + j * step, step), step)
            raw_rows_of(cc, 0, lo + j * step, step, wm[cc, rows, :], wg[cc, rows, :])

        if i == 1:
            raw_rows_of(cc, 1, WIDE, NARROW, nm[cc], ng[cc])

    def half_rows(cc, start, n):
        return pl.ds(pl.multiple_of(cc * HALF + start, 8), n)

    for copy in loads[0:6]:
        copy.wait()
    split_basis(1 - c)
    raw_set(1 - c, 0)
    pl.semaphore_wait(barrier, len(partners))
    exchanges = []
    for i, (start, n) in enumerate(sets):
        if i == 1:
            raw_set(1 - c, 1)
        exchanges.append(
            links.start(
                part.at[:, half_rows(1 - c, start, n)], swap.at[:, pl.ds(start, n)], sibling
            )
        )
    for copy in loads[6:12]:
        copy.wait()
    split_basis(c)

    x_ring = dict(q=x, right=xs[0], left=xs[2])
    y_ring = dict(q=y, right=ys[0], left=ys[2])
    base = c * HALF

    def gather_both(buffer, h, start, sizes, cuts, first, second):
        yield from ring_gather(
            links, buffer, h, start + first["q"] * sizes[0], sizes[1], cuts[1], **second
        )
        yield from ring_gather(links, buffer, h, start, sizes[0], cuts[0], **first)

    shares = []

    def whole_sum(i, h):
        start, n = sets[i]
        big, small = n // 4, n // 16
        cuts = (big // 2, (small // 16) * 8)
        first, second = (x_ring, y_ring) if h == 0 else (y_ring, x_ring)
        yield from ring_reduce(
            links, part, part, h, base + start, big, cuts[0], land=land.at[i, h, 0], **first
        )
        yield from ring_reduce(
            links, part, full, h, base + start + first["q"] * big, small, cuts[1],
            land=land.at[i, h, 1], **second
        )
        yield from gather_both(full, h, base + start, (big, small), cuts, first, second)
        done = full.at[h, half_rows(c, start, n)]
        shares.append(links.start(done, done, sibling))

    stages = []
    for i, (start, n) in enumerate(sets):
        raw_set(c, i)
        exchanges[i].wait_recv()
        rows = half_rows(c, start, n)
        part[:, rows, :] += swap[:, start : start + n, :]
        for h in range(2):
            stage = whole_sum(i, h)
            next(stage)
            stages.append(stage)
    together(*stages)

    def raw_rows(start, n):
        rows = pl.ds(pl.multiple_of(start, 8), n)
        return jnp.concatenate([full[0, rows, :], full[1, rows, :]], axis=1)

    for kind, (start, n) in enumerate(((0, WIDE), (WIDE, NARROW))):
        raw = raw_rows(base + start, n)
        gram[kind] = exact_dot(raw, raw, TN)
    places = (x * 4 + y, y * 4 + x)
    for t in range(8):
        h, m, r = t // 4, (t // 2) % 2, t % 2
        rows = pl.ds(pl.multiple_of(places[h] * 16 + r * 8, 8), 8)
        slices[t] = gram[m, rows, h * 128 : h * 128 + 128]
    gram_sends = [
        links.start(slices.at[(z + d) % 8], zland.at[d - 1], zs[d - 1]) for d in range(1, 8)
    ]

    def w_of(m):
        start, n = ((0, WIDE), (HALF, WIDE), (WIDE, NARROW), (HALF + WIDE, NARROW))[m]
        high, low = split(raw_rows(start, n))
        b_high = bh[start : start + n, :]
        w = bf16_dot(b_high, high, TN) + (
            bf16_dot(b_high, low, TN) + bf16_dot(bl[start : start + n, :], high, TN)
        )
        for k in range(8):
            wpart[k, m * 32 : m * 32 + 32, :] = w[k * 32 : k * 32 + 32, :]

    def z_chain(i):
        return z_reduce_gather(links, wpart, wfull, wland, 64 * i, 64, z, zs[0], zs[6])

    for copy in shares:
        copy.wait_recv()
    w_of(0)
    w_of(1)
    chains = [z_chain(0)]
    next(chains[0])

    def z_step():
        for chain in chains:
            next(chain, None)

    for copy in gram_sends:
        copy.wait_recv()
    total = slices[z]
    for d in range(7):
        total = total + zland[d]
    place = places[0] + (z // 4) * (places[1] - places[0])
    own = gathered.at[z // 4, pl.ds(pl.multiple_of(place * 32 + (z % 4) * 8, 8), 8)]
    own[...] = total
    gram_sends = [links.start(own, own, zs[d]) for d in range(7)]
    w_of(2)
    w_of(3)
    z_step()
    chains.append(z_chain(1))
    next(chains[1])
    for copy in gram_sends:
        copy.wait_recv()
    stages = [
        gather_both(gathered, 0, 0, (128, 32), (64, 16), x_ring, y_ring),
        gather_both(gathered, 1, 0, (128, 32), (64, 16), y_ring, x_ring),
    ]
    for i in range(5):
        for stage in stages:
            next(stage, None)
        if i in (1, 3):
            z_step()
    for h in range(2):
        for p in range(16):
            for m in range(2):
                gram[m, p * 16 : p * 16 + 16, h * 128 : h * 128 + 128] = gathered[
                    h, p * 32 + m * 16 : p * 32 + m * 16 + 16, :
                ]

    for k in range(8):
        factor_block(gram, k)
        z_step()
    full_row = lax.broadcasted_iota(jnp.int32, (256, 256), 0)
    full_col = lax.broadcasted_iota(jnp.int32, (256, 256), 1)
    for m in range(2):
        inverse[c, m] = jnp.where(full_row >= full_col, gram[m], 0.0)
    exchange = links.start(inverse.at[c], inverse.at[c], sibling)
    for chain in chains:
        for _ in chain:
            pass

    def times_inverse(a, cc, kind):
        i_high, i_low = split(inverse[cc, kind])
        high, low = split(a)
        return bf16_dot(high, i_high, NT) + (
            bf16_dot(high, i_low, NT) + bf16_dot(low, i_high, NT)
        )

    def factor_of(cc, kind):
        rows = pl.ds(pl.multiple_of(kind * 64 + cc * 32, 32), 32)
        w = jnp.concatenate([wfull[k, rows, :] for k in range(8)], axis=0)
        factor = times_inverse(w, cc, kind)
        fac[2 * kind + cc] = factor
        squares = jnp.sum(factor * factor, axis=0, keepdims=True)
        return [squares[:, 0:128], squares[:, 128:256]]

    stores = []

    def put(src, dst):
        copy = pltpu.make_async_copy(src, dst, store.at[len(stores)])
        copy.start()
        stores.append(copy)

    def ortho_half(cc):
        start = cc * HALF
        ow[cc] = times_inverse(raw_rows(start, WIDE), cc, 0)
        put(ow.at[cc], ow_out.at[cc])
        on[cc] = times_inverse(raw_rows(start + WIDE, NARROW), cc, 1)
        put(on.at[cc], on_out.at[cc])

    for kind in range(2):
        for h, squares in enumerate(factor_of(c, kind)):
            row = pl.ds(pl.multiple_of((2 * kind + c) * 2, 2) + h, 1)
            sq[row, :] = squares
    exchange.wait_recv()
    for kind in range(2):
        for h, squares in enumerate(factor_of(1 - c, kind)):
            row = pl.ds(pl.multiple_of((2 * kind + 1 - c) * 2, 2) + h, 1)
            sq[row, :] = squares
    put(fac, fac_out)
    sq_x[0] = sq[...]
    sends = [
        links.start(sq_x.at[0], sq_x.at[d + 1], device)
        for d, device in enumerate([sibling] + xs + xos)
    ]
    ortho_half(c)
    for copy in sends:
        copy.wait_recv()
    total = sq_x[0]
    for d in range(7):
        total = total + sq_x[d + 1]
    sq_y[0] = total
    sends = [links.start(sq_y.at[0], sq_y.at[d + 1], ys[d]) for d in range(3)]
    ortho_half(1 - c)
    for copy in sends:
        copy.wait_recv()
    sq[...] = sq_y[0] + sq_y[1] + sq_y[2] + sq_y[3]
    put(sq, sq_out)
    links.finish()
    for copy in stores:
        copy.wait()


def last_kernel(
    wm, wg, nm, ng, ow, on, fac, sq, wmo, wbo, wup, nmo, nbo, nup, f_t, b_high, b_low
):
    kinds = ((wm, wg, ow, wmo, wbo, wup, D), (nm, ng, on, nmo, nbo, nup, KVW))

    @pl.when(pl.program_id(1) == 0)
    def _():
        for kind in range(2):
            factor = fac[kind, 0]
            basis = factor * lax.rsqrt(sq[kind, 0] + 1e-6)
            kinds[kind][4][0] = basis
            f_t[kind] = factor.astype(BF16).T
            b_high[kind], b_low[kind] = split(basis.T)

    for kind, (moment, grad, ortho, m_out, _, update, rows) in enumerate(kinds):
        o_high, o_low = split(ortho[0])
        m_out[0] = moment[0] + grad[0].astype(F32) - 0.05 * bf16_dot(o_high, f_t[kind])
        product = bf16_dot(o_high, b_high[kind]) + (
            bf16_dot(o_high, b_low[kind]) + bf16_dot(o_low, b_high[kind])
        )
        update[0] = ((rows * D / RANK) ** 0.5 * product).astype(BF16)


def local(wide_momentum, wide_grad, wide_basis, narrow_momentum, narrow_grad, narrow_basis):
    hbm = pl.BlockSpec(memory_space=pltpu.HBM)
    copies = 144
    ow, on, fac, sq = pl.pallas_call(
        main_kernel,
        out_shape=(
            jax.ShapeDtypeStruct((2, WIDE, RANK), F32),
            jax.ShapeDtypeStruct((2, NARROW, RANK), F32),
            jax.ShapeDtypeStruct((4, COLS, RANK), F32),
            jax.ShapeDtypeStruct((8, 128), F32),
        ),
        in_specs=[hbm] * 6,
        out_specs=[hbm] * 4,
        scratch_shapes=[
            pltpu.VMEM((2, WIDE, RANK), F32),
            pltpu.VMEM((2, NARROW, RANK), F32),
            pltpu.VMEM((4, COLS, RANK), F32),
            pltpu.VMEM((8, 128), F32),
            pltpu.VMEM((2, WIDE, COLS), F32),
            pltpu.VMEM((2, WIDE, COLS), BF16),
            pltpu.VMEM((2, COLS, RANK), F32),
            pltpu.VMEM((2, NARROW, COLS), F32),
            pltpu.VMEM((2, NARROW, COLS), BF16),
            pltpu.VMEM((2, COLS, RANK), F32),
            pltpu.VMEM((2 * HALF, COLS), BF16),
            pltpu.VMEM((2 * HALF, COLS), BF16),
            pltpu.VMEM((2, 2, COLS, RANK), BF16),
            pltpu.VMEM((2, 2, COLS, RANK), BF16),
            pltpu.VMEM((2, 2 * HALF, 128), F32),
            pltpu.VMEM((2, 2 * HALF, 128), F32),
            pltpu.VMEM((2, HALF, 128), F32),
            pltpu.VMEM((2, 2, 2, 4, 160, 128), F32),
            pltpu.VMEM((2, RANK, RANK), F32),
            pltpu.VMEM((8, 8, 128), F32),
            pltpu.VMEM((7, 8, 128), F32),
            pltpu.VMEM((2, 512, 128), F32),
            pltpu.VMEM((8, 128, RANK), F32),
            pltpu.VMEM((8, 128, RANK), F32),
            pltpu.VMEM((2, 4, 128, RANK), F32),
            pltpu.VMEM((2, 2, RANK, RANK), F32),
            pltpu.VMEM((8, 8, 128), F32),
            pltpu.VMEM((4, 8, 128), F32),
            pltpu.SemaphoreType.DMA((12,)),
            pltpu.SemaphoreType.DMA((6,)),
            pltpu.SemaphoreType.DMA((copies,)),
            pltpu.SemaphoreType.DMA((copies,)),
        ],
        compiler_params=pltpu.CompilerParams(
            collective_id=0, has_side_effects=True, vmem_limit_bytes=60 * 2**20
        ),
    )(wide_momentum, wide_grad, wide_basis, narrow_momentum, narrow_grad, narrow_basis)

    def rows(n):
        return pl.BlockSpec((1, n, COLS), lambda m, i: (m, i, 0))

    def whole(*lead):
        return pl.BlockSpec(lead, lambda m, i: (0, m, 0, 0))

    basis_out = pl.BlockSpec((1, COLS, RANK), lambda m, i: (m, 0, 0))
    steps = 2
    w, n = WIDE // steps, NARROW // steps
    return pl.pallas_call(
        last_kernel,
        grid=(2, steps),
        out_shape=(
            jax.ShapeDtypeStruct((2, WIDE, COLS), F32),
            jax.ShapeDtypeStruct((2, COLS, RANK), F32),
            jax.ShapeDtypeStruct((2, WIDE, COLS), BF16),
            jax.ShapeDtypeStruct((2, NARROW, COLS), F32),
            jax.ShapeDtypeStruct((2, COLS, RANK), F32),
            jax.ShapeDtypeStruct((2, NARROW, COLS), BF16),
        ),
        in_specs=[
            rows(w), rows(w), rows(n), rows(n), rows(w), rows(n),
            whole(2, 1, COLS, RANK), whole(2, 1, 1, RANK),
        ],
        out_specs=[rows(w), basis_out, rows(w), rows(n), basis_out, rows(n)],
        scratch_shapes=[pltpu.VMEM((2, RANK, COLS), BF16)] * 3,
        compiler_params=pltpu.CompilerParams(vmem_limit_bytes=60 * 2**20),
    )(
        wide_momentum, wide_grad, narrow_momentum, narrow_grad, ow, on,
        fac.reshape(2, 2, COLS, RANK), sq.reshape(2, 2, 1, RANK),
    )


def solution(mesh):
    return jax.shard_map(
        local,
        mesh=mesh,
        in_specs=(
            P(None, "mp", "fsdp"),
            P(None, "mp", "fsdp"),
            P(None, "fsdp", None),
            P(None, "mp", "fsdp"),
            P(None, "mp", "fsdp"),
            P(None, "fsdp", None),
        ),
        out_specs=(
            P(None, "mp", "fsdp"),
            P(None, "fsdp", None),
            P(None, "mp", "fsdp"),
            P(None, "mp", "fsdp"),
            P(None, "fsdp", None),
            P(None, "mp", "fsdp"),
        ),
        check_vma=False,
    )
```

time: 127 us -> 110 us (0.87)
  Pallas kernels: 121 us -> 109 us
  local copies, waits for them, and re-layouts: 5.31 us -> 0 us
    pallas_call x1, Pallas kernels: 116 us -> 102 us  [local(): pl.pallas_call(main_kernel, out_shape=(jax.ShapeDtypeStruct((2, WIDE, RAN...]
    unnamed x12 -> x0, local copies, waits for them, and re-layouts: 5.31 us -> none
    pallas_call x1, Pallas kernels: 5.3 us -> 6.96 us  [local(): pl.pallas_call(last_kernel, grid=(2, steps), out_shape=(jax.ShapeDtypeStr...]
where the time goes in v2:
time: 110 us; the launch traced here: 109 us
  Pallas kernels  109 us (99%)
    pallas_call x1, Pallas kernels, local(): pl.pallas_call(main_kernel, out_shape=(jax.ShapeDtypeStruct((2, WIDE, RAN...  102 us
    pallas_call x1, Pallas kernels, local(): pl.pallas_call(last_kernel, grid=(2, steps), out_shape=(jax.ShapeDtypeStr...  6.96 us

profile of v2, /device:TPU:1, one launch (start us, length us, event | category | flops | bytes accessed | tf_op | source)
XLA Modules:
  0.0 109.4 jit_solution(531716656326442852)
XLA Ops:
  0.6 101.8 %shard_map.109 = (f32[2,1024,256]{2,1,0:T(8,128)}, f32[2,128,256]{2,1,0:T(8,128)}, f32[4,256,256]{2,1,0:T(8,128)}, f32[8,128]{1,0:T(8,128)}) custom-call(f32[2,1024,256]{2,1,0:T(8,128)} %wm.1, bf16[2,1024,256]{2,1,0:T(8,128)(2,1)} %wg.1, f32[2,256,256]{2,1,0:T(8,128)} %wb_in.1, f32[2,128,256]{2,1,0:T(8,128)} %nm.1, bf16[2,128,256]{2,1,0:T(8,128)(2,1)} %ng.1, ...), custom_call_target="tpu_custom_call" | custom-call | tf_op jit(solution)/shard_map/pallas_call | solution.py:532
  102.4 7.0 %shard_map.110 = (f32[2,1024,256]{2,1,0:T(8,128)}, f32[2,256,256]{2,1,0:T(8,128)}, bf16[2,1024,256]{2,1,0:T(8,128)(2,1)}, f32[2,128,256]{2,1,0:T(8,128)}, f32[2,...) custom-call(f32[2,1024,256]{2,1,0:T(8,128)} %wm.1, bf16[2,1024,256]{2,1,0:T(8,128)(2,1)} %wg.1, f32[2,128,256]{2,1,0:T(8,128)} %nm.1, ...), custom_call_target="tpu_custom_call" | custom-call | tf_op jit(solution)/shard_map/pallas_call | solution.py:590

commit v3 on v2

--- a/solution.py
+++ b/solution.py
@@ -56,13 +56,16 @@
         self.started.append(copy)
         return copy
 
-    def finish(self):
-        for copy in self.started:
+    def finish(self, most=None):
+        n = len(self.started) if most is None else most
+        for copy in self.started[:n]:
             copy.wait_send()
-
-
-def ring_reduce(links, buf, out, h, base, chunk, cut, q, right, left, land):
+        self.started = self.started[n:]
+
+
+def ring_reduce(links, buf, out, h, base, chunk, cut, q, peers, land):
     after, before = (q + 1) % 4, (q + 3) % 4
+    right, left = peers[0], peers[2]
 
     def rows(c, lo, n):
         return pl.ds(pl.multiple_of(base + c * chunk + lo, 8), n)
@@ -87,8 +90,9 @@
     )
 
 
-def ring_gather(links, buf, h, base, chunk, cut, q, right, left):
+def ring_gather(links, buf, h, base, chunk, cut, q, peers):
     after, before = (q + 1) % 4, (q + 3) % 4
+    right, left = peers[0], peers[2]
 
     def part(c, lo, n):
         return buf.at[h, pl.ds(pl.multiple_of(base + c * chunk + lo, 8), n)]
@@ -106,6 +110,31 @@
     yield
     a.wait_recv()
     b.wait_recv()
+
+
+def direct_reduce(links, buf, out, h, base, chunk, q, peers, land):
+    def rows(c):
+        return pl.ds(pl.multiple_of(base + c * chunk, 8), chunk)
+
+    copies = [
+        links.start(buf.at[h, rows((q + d) % 4)], land.at[d, pl.ds(0, chunk)], peers[d - 1])
+        for d in (2, 1, 3)
+    ]
+    yield
+    for copy in copies:
+        copy.wait_recv()
+    total = buf[h, rows(q), :]
+    for d in (1, 2, 3):
+        total = total + land[d, 0:chunk, :]
+    out[h, rows(q), :] = total
+
+
+def direct_gather(links, buf, h, base, chunk, q, peers):
+    own = buf.at[h, pl.ds(pl.multiple_of(base + q * chunk, 8), chunk)]
+    copies = [links.start(own, own, peers[d - 1]) for d in (2, 1, 3)]
+    yield
+    for copy in copies:
+        copy.wait_recv()
 
 
 def z_reduce_gather(links, buf, out, land, lo, n, q, right, left):
@@ -161,11 +190,15 @@
     b.wait_recv()
 
 
-def together(*stages):
+def together(first, second, after):
     done = object()
-    live = list(stages)
-    while live:
-        live = [s for s in live if next(s, done) is not done]
+    ended = False
+    while first or second:
+        first = [s for s in first if next(s, done) is not done]
+        if not first and not ended:
+            after()
+            ended = True
+        second = [s for s in second if next(s, done) is not done]
 
 
 def block_inverse(e):
@@ -228,13 +261,11 @@
 
 
 def main_kernel(
-    wm_in, wg_in, wb_in, nm_in, ng_in, nb_in,
-    ow_out, on_out, fac_out, sq_out,
+    bw, bn, wb, nb,
     ow, on, fac, sq,
-    wm, wg, wb, nm, ng, nb,
     bh, bl, vh, vl, part, full, swap, land, gram, slices, zland, gathered,
     wpart, wfull, wland, inverse, sq_x, sq_y,
-    load, store, send, recv,
+    send, recv,
 ):
     z = lax.axis_index("mp")
     f = lax.axis_index("fsdp")
@@ -242,14 +273,6 @@
     x = (f // 2) % 4
     y = f // 8
 
-    loads = []
-    for i, cc in enumerate((1 - c, c)):
-        pairs = ((wb_in, wb), (wg_in, wg), (wm_in, wm), (nb_in, nb), (ng_in, ng), (nm_in, nm))
-        for n, (src, dst) in enumerate(pairs):
-            copy = pltpu.make_async_copy(src.at[cc], dst.at[cc], load.at[6 * i + n])
-            copy.start()
-            loads.append(copy)
-
     def plane(xx, yy, cc):
         return {"fsdp": ((yy % 4) * 4 + xx % 4) * 2 + cc}
 
@@ -274,9 +297,9 @@
             vh[cc, kind] = high
             vl[cc, kind] = low
 
-    def raw_rows_of(cc, kind, r, n, moment, grad):
+    def raw_rows_of(cc, kind, r, n, buffer):
         rows = pl.ds(pl.multiple_of(cc * HALF + r, 16), n)
-        high, low = split(moment + grad.astype(F32))
+        high, low = split(buffer)
         bh[rows, :] = high
         bl[rows, :] = low
         v_high = vh[cc, kind]
@@ -291,16 +314,14 @@
         @pl.loop(0, n // step)
         def _(j):
             rows = pl.ds(pl.multiple_of(lo + j * step, step), step)
-            raw_rows_of(cc, 0, lo + j * step, step, wm[cc, rows, :], wg[cc, rows, :])
+            raw_rows_of(cc, 0, lo + j * step, step, bw[cc, rows, :])
 
         if i == 1:
-            raw_rows_of(cc, 1, WIDE, NARROW, nm[cc], ng[cc])
+            raw_rows_of(cc, 1, WIDE, NARROW, bn[cc])
 
     def half_rows(cc, start, n):
         return pl.ds(pl.multiple_of(cc * HALF + start, 8), n)
 
-    for copy in loads[0:6]:
-        copy.wait()
     split_basis(1 - c)
     raw_set(1 - c, 0)
     pl.semaphore_wait(barrier, len(partners))
@@ -313,35 +334,32 @@
                 part.at[:, half_rows(1 - c, start, n)], swap.at[:, pl.ds(start, n)], sibling
             )
         )
-    for copy in loads[6:12]:
-        copy.wait()
     split_basis(c)
 
-    x_ring = dict(q=x, right=xs[0], left=xs[2])
-    y_ring = dict(q=y, right=ys[0], left=ys[2])
+    x_ring = dict(q=x, peers=xs)
+    y_ring = dict(q=y, peers=ys)
     base = c * HALF
 
-    def gather_both(buffer, h, start, sizes, cuts, first, second):
-        yield from ring_gather(
-            links, buffer, h, start + first["q"] * sizes[0], sizes[1], cuts[1], **second
-        )
-        yield from ring_gather(links, buffer, h, start, sizes[0], cuts[0], **first)
+    def gather_both(buffer, h, start, sizes, first, second):
+        yield from direct_gather(
+            links, buffer, h, start + first["q"] * sizes[0], sizes[1], **second
+        )
+        yield from ring_gather(links, buffer, h, start, sizes[0], sizes[0] // 2, **first)
 
     shares = []
 
     def whole_sum(i, h):
         start, n = sets[i]
         big, small = n // 4, n // 16
-        cuts = (big // 2, (small // 16) * 8)
         first, second = (x_ring, y_ring) if h == 0 else (y_ring, x_ring)
         yield from ring_reduce(
-            links, part, part, h, base + start, big, cuts[0], land=land.at[i, h, 0], **first
-        )
-        yield from ring_reduce(
-            links, part, full, h, base + start + first["q"] * big, small, cuts[1],
+            links, part, part, h, base + start, big, big // 2, land=land.at[i, h, 0], **first
+        )
+        yield from direct_reduce(
+            links, part, full, h, base + start + first["q"] * big, small,
             land=land.at[i, h, 1], **second
         )
-        yield from gather_both(full, h, base + start, (big, small), cuts, first, second)
+        yield from gather_both(full, h, base + start, (big, small), first, second)
         done = full.at[h, half_rows(c, start, n)]
         shares.append(links.start(done, done, sibling))
 
@@ -355,15 +373,19 @@
             stage = whole_sum(i, h)
             next(stage)
             stages.append(stage)
-    together(*stages)
 
     def raw_rows(start, n):
         rows = pl.ds(pl.multiple_of(start, 8), n)
         return jnp.concatenate([full[0, rows, :], full[1, rows, :]], axis=1)
 
-    for kind, (start, n) in enumerate(((0, WIDE), (WIDE, NARROW))):
+    def own_gram(start, n):
         raw = raw_rows(base + start, n)
-        gram[kind] = exact_dot(raw, raw, TN)
+        return exact_dot(raw, raw, TN)
+
+    together(stages[0:2], stages[2:4], after=lambda: gram.__setitem__(0, own_gram(0, 640)))
+    gram[0] += own_gram(640, wide_b)
+    gram[1] = own_gram(WIDE, NARROW)
+
     places = (x * 4 + y, y * 4 + x)
     for t in range(8):
         h, m, r = t // 4, (t // 2) % 2, t % 2
@@ -414,13 +436,15 @@
     for copy in gram_sends:
         copy.wait_recv()
     stages = [
-        gather_both(gathered, 0, 0, (128, 32), (64, 16), x_ring, y_ring),
-        gather_both(gathered, 1, 0, (128, 32), (64, 16), y_ring, x_ring),
+        gather_both(gathered, 0, 0, (128, 32), x_ring, y_ring),
+        gather_both(gathered, 1, 0, (128, 32), y_ring, x_ring),
     ]
-    for i in range(5):
+    for i in range(4):
         for stage in stages:
             next(stage, None)
-        if i in (1, 3):
+        if i < 3:
+            links.finish(36)
+        if i in (1, 2):
             z_step()
     for h in range(2):
         for p in range(16):
@@ -456,19 +480,10 @@
         squares = jnp.sum(factor * factor, axis=0, keepdims=True)
         return [squares[:, 0:128], squares[:, 128:256]]
 
-    stores = []
-
-    def put(src, dst):
-        copy = pltpu.make_async_copy(src, dst, store.at[len(stores)])
-        copy.start()
-        stores.append(copy)
-
     def ortho_half(cc):
         start = cc * HALF
         ow[cc] = times_inverse(raw_rows(start, WIDE), cc, 0)
-        put(ow.at[cc], ow_out.at[cc])
         on[cc] = times_inverse(raw_rows(start + WIDE, NARROW), cc, 1)
-        put(on.at[cc], on_out.at[cc])
 
     for kind in range(2):
         for h, squares in enumerate(factor_of(c, kind)):
@@ -479,7 +494,6 @@
         for h, squares in enumerate(factor_of(1 - c, kind)):
             row = pl.ds(pl.multiple_of((2 * kind + 1 - c) * 2, 2) + h, 1)
             sq[row, :] = squares
-    put(fac, fac_out)
     sq_x[0] = sq[...]
     sends = [
         links.start(sq_x.at[0], sq_x.at[d + 1], device)
@@ -497,29 +511,26 @@
     for copy in sends:
         copy.wait_recv()
     sq[...] = sq_y[0] + sq_y[1] + sq_y[2] + sq_y[3]
-    put(sq, sq_out)
     links.finish()
-    for copy in stores:
-        copy.wait()
 
 
 def last_kernel(
-    wm, wg, nm, ng, ow, on, fac, sq, wmo, wbo, wup, nmo, nbo, nup, f_t, b_high, b_low
+    bw, bn, ow, on, fac, sq, wmo, wbo, wup, nmo, nbo, nup, f_t, b_high, b_low
 ):
-    kinds = ((wm, wg, ow, wmo, wbo, wup, D), (nm, ng, on, nmo, nbo, nup, KVW))
+    kinds = ((bw, ow, wmo, wbo, wup, D), (bn, on, nmo, nbo, nup, KVW))
 
     @pl.when(pl.program_id(1) == 0)
     def _():
         for kind in range(2):
             factor = fac[kind, 0]
             basis = factor * lax.rsqrt(sq[kind, 0] + 1e-6)
-            kinds[kind][4][0] = basis
+            kinds[kind][3][0] = basis
             f_t[kind] = factor.astype(BF16).T
             b_high[kind], b_low[kind] = split(basis.T)
 
-    for kind, (moment, grad, ortho, m_out, _, update, rows) in enumerate(kinds):
+    for kind, (buffer, ortho, m_out, _, update, rows) in enumerate(kinds):
         o_high, o_low = split(ortho[0])
-        m_out[0] = moment[0] + grad[0].astype(F32) - 0.05 * bf16_dot(o_high, f_t[kind])
+        m_out[0] = buffer[0] - 0.05 * bf16_dot(o_high, f_t[kind])
         product = bf16_dot(o_high, b_high[kind]) + (
             bf16_dot(o_high, b_low[kind]) + bf16_dot(o_low, b_high[kind])
         )
@@ -527,7 +538,9 @@
 
 
 def local(wide_momentum, wide_grad, wide_basis, narrow_momentum, narrow_grad, narrow_basis):
-    hbm = pl.BlockSpec(memory_space=pltpu.HBM)
+    vmem = pl.BlockSpec(memory_space=pltpu.VMEM)
+    bw = wide_momentum + wide_grad.astype(F32)
+    bn = narrow_momentum + narrow_grad.astype(F32)
     copies = 144
     ow, on, fac, sq = pl.pallas_call(
         main_kernel,
@@ -537,19 +550,9 @@
             jax.ShapeDtypeStruct((4, COLS, RANK), F32),
             jax.ShapeDtypeStruct((8, 128), F32),
         ),
-        in_specs=[hbm] * 6,
-        out_specs=[hbm] * 4,
+        in_specs=[vmem] * 4,
+        out_specs=[vmem] * 4,
         scratch_shapes=[
-            pltpu.VMEM((2, WIDE, RANK), F32),
-            pltpu.VMEM((2, NARROW, RANK), F32),
-            pltpu.VMEM((4, COLS, RANK), F32),
-            pltpu.VMEM((8, 128), F32),
-            pltpu.VMEM((2, WIDE, COLS), F32),
-            pltpu.VMEM((2, WIDE, COLS), BF16),
-            pltpu.VMEM((2, COLS, RANK), F32),
-            pltpu.VMEM((2, NARROW, COLS), F32),
-            pltpu.VMEM((2, NARROW, COLS), BF16),
-            pltpu.VMEM((2, COLS, RANK), F32),
             pltpu.VMEM((2 * HALF, COLS), BF16),
             pltpu.VMEM((2 * HALF, COLS), BF16),
             pltpu.VMEM((2, 2, COLS, RANK), BF16),
@@ -568,15 +571,13 @@
             pltpu.VMEM((2, 2, RANK, RANK), F32),
             pltpu.VMEM((8, 8, 128), F32),
             pltpu.VMEM((4, 8, 128), F32),
-            pltpu.SemaphoreType.DMA((12,)),
-            pltpu.SemaphoreType.DMA((6,)),
             pltpu.SemaphoreType.DMA((copies,)),
             pltpu.SemaphoreType.DMA((copies,)),
         ],
         compiler_params=pltpu.CompilerParams(
-            collective_id=0, has_side_effects=True, vmem_limit_bytes=60 * 2**20
+            collective_id=0, has_side_effects=True, vmem_limit_bytes=36 * 2**20
         ),
-    )(wide_momentum, wide_grad, wide_basis, narrow_momentum, narrow_grad, narrow_basis)
+    )(bw, bn, wide_basis, narrow_basis)
 
     def rows(n):
         return pl.BlockSpec((1, n, COLS), lambda m, i: (m, i, 0))
@@ -599,14 +600,14 @@
             jax.ShapeDtypeStruct((2, NARROW, COLS), BF16),
         ),
         in_specs=[
-            rows(w), rows(w), rows(n), rows(n), rows(w), rows(n),
+            rows(w), rows(n), rows(w), rows(n),
             whole(2, 1, COLS, RANK), whole(2, 1, 1, RANK),
         ],
         out_specs=[rows(w), basis_out, rows(w), rows(n), basis_out, rows(n)],
         scratch_shapes=[pltpu.VMEM((2, RANK, COLS), BF16)] * 3,
-        compiler_params=pltpu.CompilerParams(vmem_limit_bytes=60 * 2**20),
+        compiler_params=pltpu.CompilerParams(vmem_limit_bytes=24 * 2**20),
     )(
-        wide_momentum, wide_grad, narrow_momentum, narrow_grad, ow, on,
+        bw, bn, ow, on,
         fac.reshape(2, 2, COLS, RANK), sq.reshape(2, 2, 1, RANK),
     )
 

time: 110 us -> 101 us (0.918)
  Pallas kernels: 109 us -> 97.4 us
  other arithmetic: 0 us -> 3.16 us
    pallas_call x1, Pallas kernels: 102 us -> 93.3 us  [local(): pl.pallas_call(main_kernel, out_shape=(jax.ShapeDtypeStruct((2, WIDE, RAN...]
    add x0 -> x2, other arithmetic: none -> 3.16 us  [the longest x1 2.15 us: local(): bw = wide_momentum + wide_grad.astype(F32)]
    pallas_call x1, Pallas kernels: 6.96 us -> 4.1 us  [local(): pl.pallas_call(last_kernel, grid=(2, steps), out_shape=(jax.ShapeDtypeStr...]
where the time goes in v3:
time: 101 us
  Pallas kernels  97.4 us (96%)
  other arithmetic  3.16 us (3%)
    pallas_call x1, Pallas kernels, local(): pl.pallas_call(main_kernel, out_shape=(jax.ShapeDtypeStruct((2, WIDE, RAN...  93.3 us
    pallas_call x1, Pallas kernels, local(): pl.pallas_call(last_kernel, grid=(2, steps), out_shape=(jax.ShapeDtypeStr...  4.1 us
    add x1, other arithmetic, local(): bw = wide_momentum + wide_grad.astype(F32)  2.15 us

profile of v3, /device:TPU:1, one launch (start us, length us, event | category | flops | bytes accessed | tf_op | source)
XLA Modules:
  0.0 101.2 jit_solution(13287656209838952166)
XLA Ops:
  0.6 1.0 convert_add_fusion.1.bn
  1.6 0.0 copy-start
  1.7 0.0 copy-start.1
  1.7 2.2 %convert_add_fusion.bw = f32[2,1024,256]{2,1,0:T(8,128)S(1)} fusion(f32[2,1024,256]{2,1,0:T(8,128)} %param.6, bf16[2,1024,256]{2,1,0:T(8,128)(2,1)} %param.7), kind=kLoop, calls=%fused_computation | loop fusion | flops 1048576 | bytes 5242880 | tf_op jit(solution)/shard_map/add | solution.py:542
  3.8 0.0 copy-done
  3.8 0.0 copy-done.1
  3.8 93.3 %shard_map.109 = (f32[2,1024,256]{2,1,0:T(8,128)S(1)}, f32[2,128,256]{2,1,0:T(8,128)S(1)}, f32[4,256,256]{2,1,0:T(8,128)S(1)}, f32[8,128]{1,0:T(8,128)S(1)}) custom-call(f32[2,1024,256]{2,1,0:T(8,128)S(1)} %convert_add_fusion.bw, f32[2,128,256]{2,1,0:T(8,128)S(1)} %convert_add_fusion.1.bn, f32[2,256,256]{2,1,0:T(8,128)S(1)} %copy-done, ...), custom_call_target="tpu_custom_call" | custom-call | tf_op jit(solution)/shard_map/pallas_call | solution.py:545
  97.1 4.1 %shard_map.110 = (f32[2,1024,256]{2,1,0:T(8,128)}, f32[2,256,256]{2,1,0:T(8,128)}, bf16[2,1024,256]{2,1,0:T(8,128)(2,1)}, f32[2,128,256]{2,1,0:T(8,128)}, f32[2,...) custom-call(f32[2,1024,256]{2,1,0:T(8,128)S(1)} %convert_add_fusion.bw, f32[2,128,256]{2,1,0:T(8,128)S(1)} %convert_add_fusion.1.bn, ...), custom_call_target="tpu_custom_call" | custom-call | tf_op jit(solution)/shard_map/pallas_call | solution.py:591
Async XLA Ops:
  1.6 2.2 %copy-start = (f32[2,256,256]{2,1,0:T(8,128)S(1)}, f32[2,256,256]{2,1,0:T(8,128)}, u32[]{:S(2)}) copy-start(f32[2,256,256]{2,1,0:T(8,128)} %wb.1) | copy-start | bytes 1572868
  1.7 2.2 %copy-start.1 = (f32[2,256,256]{2,1,0:T(8,128)S(1)}, f32[2,256,256]{2,1,0:T(8,128)}, u32[]{:S(2)}) copy-start(f32[2,256,256]{2,1,0:T(8,128)} %nb.1) | copy-start | bytes 1572868

commit v4 on v3

--- a/solution.py
+++ b/solution.py
@@ -263,7 +263,7 @@
 def main_kernel(
     bw, bn, wb, nb,
     ow, on, fac, sq,
-    bh, bl, vh, vl, part, full, swap, land, gram, slices, zland, gathered,
+    bh, bl, vh, vl, part, full, swap, land, gram, cross, w_first, slices, zland, gathered,
     wpart, wfull, wland, inverse, sq_x, sq_y,
     send, recv,
 ):
@@ -309,12 +309,7 @@
 
     def raw_set(cc, i):
         lo, n = ((0, 640), (640, wide_b))[i]
-        step = 128
-
-        @pl.loop(0, n // step)
-        def _(j):
-            rows = pl.ds(pl.multiple_of(lo + j * step, step), step)
-            raw_rows_of(cc, 0, lo + j * step, step, bw[cc, rows, :])
+        raw_rows_of(cc, 0, lo, n, bw[cc, lo : lo + n, :])
 
         if i == 1:
             raw_rows_of(cc, 1, WIDE, NARROW, bn[cc])
@@ -380,9 +375,26 @@
 
     def own_gram(start, n):
         raw = raw_rows(base + start, n)
-        return exact_dot(raw, raw, TN)
-
-    together(stages[0:2], stages[2:4], after=lambda: gram.__setitem__(0, own_gram(0, 640)))
+        high = raw.astype(BF16)
+        middle, low = split(raw - high.astype(F32))
+        cross[...] = bf16_dot(high, middle, TN) + bf16_dot(high, low, TN)
+        mirrored = cross[...] + cross[...].T
+        return bf16_dot(high, high, TN) + (mirrored + bf16_dot(middle, middle, TN))
+
+    def w_of(cc, start, n):
+        start = cc * HALF + start
+        rows = pl.ds(pl.multiple_of(start, 16), n)
+        high, low = split(raw_rows(start, n))
+        b_high = bh[rows, :]
+        return bf16_dot(b_high, high, TN) + (
+            bf16_dot(b_high, low, TN) + bf16_dot(bl[rows, :], high, TN)
+        )
+
+    def first_set():
+        gram[0] = own_gram(0, 640)
+        w_first[...] = w_of(c, 0, 640)
+
+    together(stages[0:2], stages[2:4], after=first_set)
     gram[0] += own_gram(640, wide_b)
     gram[1] = own_gram(WIDE, NARROW)
 
@@ -395,23 +407,16 @@
         links.start(slices.at[(z + d) % 8], zland.at[d - 1], zs[d - 1]) for d in range(1, 8)
     ]
 
-    def w_of(m):
-        start, n = ((0, WIDE), (HALF, WIDE), (WIDE, NARROW), (HALF + WIDE, NARROW))[m]
-        high, low = split(raw_rows(start, n))
-        b_high = bh[start : start + n, :]
-        w = bf16_dot(b_high, high, TN) + (
-            bf16_dot(b_high, low, TN) + bf16_dot(bl[start : start + n, :], high, TN)
-        )
+    def put_w(i, kind, w):
+        row = i * 64 + kind * 32
         for k in range(8):
-            wpart[k, m * 32 : m * 32 + 32, :] = w[k * 32 : k * 32 + 32, :]
+            wpart[k, row : row + 32, :] = w[k * 32 : k * 32 + 32, :]
 
     def z_chain(i):
         return z_reduce_gather(links, wpart, wfull, wland, 64 * i, 64, z, zs[0], zs[6])
 
-    for copy in shares:
-        copy.wait_recv()
-    w_of(0)
-    w_of(1)
+    put_w(0, 0, w_first[...] + w_of(c, 640, wide_b))
+    put_w(0, 1, w_of(c, WIDE, NARROW))
     chains = [z_chain(0)]
     next(chains[0])
 
@@ -428,8 +433,10 @@
     own = gathered.at[z // 4, pl.ds(pl.multiple_of(place * 32 + (z % 4) * 8, 8), 8)]
     own[...] = total
     gram_sends = [links.start(own, own, zs[d]) for d in range(7)]
-    w_of(2)
-    w_of(3)
+    for copy in shares:
+        copy.wait_recv()
+    put_w(1, 0, w_of(1 - c, 0, WIDE))
+    put_w(1, 1, w_of(1 - c, WIDE, NARROW))
     z_step()
     chains.append(z_chain(1))
     next(chains[1])
@@ -444,8 +451,7 @@
             next(stage, None)
         if i < 3:
             links.finish(36)
-        if i in (1, 2):
-            z_step()
+        z_step()
     for h in range(2):
         for p in range(16):
             for m in range(2):
@@ -455,7 +461,8 @@
 
     for k in range(8):
         factor_block(gram, k)
-        z_step()
+        if k % 2:
+            z_step()
     full_row = lax.broadcasted_iota(jnp.int32, (256, 256), 0)
     full_col = lax.broadcasted_iota(jnp.int32, (256, 256), 1)
     for m in range(2):
@@ -472,9 +479,9 @@
             bf16_dot(high, i_low, NT) + bf16_dot(low, i_high, NT)
         )
 
-    def factor_of(cc, kind):
-        rows = pl.ds(pl.multiple_of(kind * 64 + cc * 32, 32), 32)
-        w = jnp.concatenate([wfull[k, rows, :] for k in range(8)], axis=0)
+    def factor_of(i, cc, kind):
+        row = i * 64 + kind * 32
+        w = jnp.concatenate([wfull[k, row : row + 32, :] for k in range(8)], axis=0)
         factor = times_inverse(w, cc, kind)
         fac[2 * kind + cc] = factor
         squares = jnp.sum(factor * factor, axis=0, keepdims=True)
@@ -486,12 +493,12 @@
         on[cc] = times_inverse(raw_rows(start + WIDE, NARROW), cc, 1)
 
     for kind in range(2):
-        for h, squares in enumerate(factor_of(c, kind)):
+        for h, squares in enumerate(factor_of(0, c, kind)):
             row = pl.ds(pl.multiple_of((2 * kind + c) * 2, 2) + h, 1)
             sq[row, :] = squares
     exchange.wait_recv()
     for kind in range(2):
-        for h, squares in enumerate(factor_of(1 - c, kind)):
+        for h, squares in enumerate(factor_of(1, 1 - c, kind)):
             row = pl.ds(pl.multiple_of((2 * kind + 1 - c) * 2, 2) + h, 1)
             sq[row, :] = squares
     sq_x[0] = sq[...]
@@ -562,6 +569,8 @@
             pltpu.VMEM((2, HALF, 128), F32),
             pltpu.VMEM((2, 2, 2, 4, 160, 128), F32),
             pltpu.VMEM((2, RANK, RANK), F32),
+            pltpu.VMEM((RANK, RANK), F32),
+            pltpu.VMEM((COLS, RANK), F32),
             pltpu.VMEM((8, 8, 128), F32),
             pltpu.VMEM((7, 8, 128), F32),
             pltpu.VMEM((2, 512, 128), F32),

time: 101 us -> 96.6 us (0.956)
  Pallas kernels: 97.4 us -> 92.5 us
    pallas_call x1, Pallas kernels: 93.3 us -> 88.4 us  [local(): pl.pallas_call(main_kernel, out_shape=(jax.ShapeDtypeStruct((2, WIDE, RAN...]
where the time goes in v4:
time: 96.6 us; the launch traced here: 96.5 us
  Pallas kernels  92.5 us (96%)
  other arithmetic  3.16 us (3%)
    pallas_call x1, Pallas kernels, local(): pl.pallas_call(main_kernel, out_shape=(jax.ShapeDtypeStruct((2, WIDE, RAN...  88.4 us
    pallas_call x1, Pallas kernels, local(): pl.pallas_call(last_kernel, grid=(2, steps), out_shape=(jax.ShapeDtypeStr...  4.1 us
    add x1, other arithmetic, local(): bw = wide_momentum + wide_grad.astype(F32)  2.15 us

profile of v4, /device:TPU:1, one launch (start us, length us, event | category | flops | bytes accessed | tf_op | source)
XLA Modules:
  0.0 96.5 jit_solution(1932552248688047151)
XLA Ops:
  0.6 1.0 %convert_add_fusion.1.bn = f32[2,128,256]{2,1,0:T(8,128)S(1)} fusion(f32[2,128,256]{2,1,0:T(8,128)} %param.9, bf16[2,128,256]{2,1,0:T(8,128)(2,1)} %param.10), kind=kLoop, calls=%fused_computation.1 | loop fusion | flops 131072 | bytes 655360 | tf_op jit(solution)/shard_map/add | solution.py:550
  1.6 0.0 copy-start
  1.7 0.0 copy-start.1
  1.7 2.2 %convert_add_fusion.bw = f32[2,1024,256]{2,1,0:T(8,128)S(1)} fusion(f32[2,1024,256]{2,1,0:T(8,128)} %param.6, bf16[2,1024,256]{2,1,0:T(8,128)(2,1)} %param.7), kind=kLoop, calls=%fused_computation | loop fusion | flops 1048576 | bytes 5242880 | tf_op jit(solution)/shard_map/add | solution.py:549
  3.8 0.0 copy-done
  3.8 0.0 copy-done.1
  3.8 88.4 %shard_map.109 = (f32[2,1024,256]{2,1,0:T(8,128)S(1)}, f32[2,128,256]{2,1,0:T(8,128)S(1)}, f32[4,256,256]{2,1,0:T(8,128)S(1)}, f32[8,128]{1,0:T(8,128)S(1)}) custom-call(f32[2,1024,256]{2,1,0:T(8,128)S(1)} %convert_add_fusion.bw, f32[2,128,256]{2,1,0:T(8,128)S(1)} %convert_add_fusion.1.bn, f32[2,256,256]{2,1,0:T(8,128)S(1)} %copy-done, ...), custom_call_target="tpu_custom_call" | custom-call | tf_op jit(solution)/shard_map/pallas_call | solution.py:552
  92.3 4.1 %shard_map.110 = (f32[2,1024,256]{2,1,0:T(8,128)}, f32[2,256,256]{2,1,0:T(8,128)}, bf16[2,1024,256]{2,1,0:T(8,128)(2,1)}, f32[2,128,256]{2,1,0:T(8,128)}, f32[2,...) custom-call(f32[2,1024,256]{2,1,0:T(8,128)S(1)} %convert_add_fusion.bw, f32[2,128,256]{2,1,0:T(8,128)S(1)} %convert_add_fusion.1.bn, ...), custom_call_target="tpu_custom_call" | custom-call | tf_op jit(solution)/shard_map/pallas_call | solution.py:600
Async XLA Ops:
  1.6 2.2 %copy-start = (f32[2,256,256]{2,1,0:T(8,128)S(1)}, f32[2,256,256]{2,1,0:T(8,128)}, u32[]{:S(2)}) copy-start(f32[2,256,256]{2,1,0:T(8,128)} %wb.1) | copy-start | bytes 1572868
  1.7 2.2 %copy-start.1 = (f32[2,256,256]{2,1,0:T(8,128)S(1)}, f32[2,256,256]{2,1,0:T(8,128)}, u32[]{:S(2)}) copy-start(f32[2,256,256]{2,1,0:T(8,128)} %nb.1) | copy-start | bytes 1572868

commit v5 on v4

--- a/solution.py
+++ b/solution.py
@@ -226,45 +226,58 @@
     return [tile * lax.rsqrt(pick(tile, 8 * i + sub)) for i, tile in enumerate(e)]
 
 
-def factor_block(a_ref, k):
-    at = 32 * k
-    base = at // 128 * 128
-    off = at - base
+def invert_factor(a_ref, out, after):
     lane = lax.broadcasted_iota(jnp.int32, (32, 128), 1)
     row = lax.broadcasted_iota(jnp.int32, (32, 128), 0)
     eye = jnp.where(lane % 32 == row, 1.0, 0.0)
+    col = lax.broadcasted_iota(jnp.int32, (32, 256), 1)
+    wide_row = lax.broadcasted_iota(jnp.int32, (32, 256), 0)
 
     def turned(v, by):
         return pltpu.roll(v, by % 128, 1) if by % 128 else v
 
-    d0, d1 = (a_ref[m, at : at + 32, base : base + 128] for m in range(2))
-    d0, d1 = turned(d0, -off), turned(d1, 64 - off)
-    e = jnp.where(lane < 32, d0, jnp.where((lane >= 64) & (lane < 96), d1, eye))
-    e = jnp.concatenate(block_inverse([e[8 * i : 8 * i + 8] for i in range(4)]), axis=0)
-    col = lax.broadcasted_iota(jnp.int32, (32, 256), 1)
-    wide_row = lax.broadcasted_iota(jnp.int32, (32, 256), 0)
-    inside = (col >= at) & (col < at + 32)
-    wide_eye = jnp.where(col - at == wide_row, 1.0, 0.0)
-    below = at + 32
-    low = below // 128 * 128
-    for m in range(2):
-        t = turned(e, 96 - 64 * m)[:, 0:32]
-        panel = exact_dot(t, jnp.where(inside, wide_eye, a_ref[m, at : at + 32, :]))
-        a_ref[m, at : at + 32, :] = panel
-        if below < 256:
-            change = exact_dot(panel[:, low:256], panel, TN)
-            under = lax.broadcasted_iota(jnp.int32, (256 - below, 256), 1)
-            rest = jnp.where(
-                (under >= at) & (under < below), 0.0, a_ref[m, below:256, :]
-            )
-            a_ref[m, below:256, :] = rest - change[below - low :, :]
+    blocks = [a_ref[m, 0:32, 0:128] for m in range(2)]
+    panels = None
+    for k in range(8):
+        at, below = 32 * k, 32 * k + 32
+        base, low = at // 128 * 128, below // 128 * 128
+        if k > 0:
+            for m in range(2):
+                change = exact_dot(panels[m][:, base:256], panels[m], TN)
+                under = lax.broadcasted_iota(jnp.int32, (256 - at, 256), 1)
+                rest = jnp.where(
+                    (under >= at - 32) & (under < at), 0.0, a_ref[m, at:256, :]
+                )
+                a_ref[m, at:256, :] = rest - change[at - base :, :]
+        d0, d1 = turned(blocks[0], base - at), turned(blocks[1], 64 + base - at)
+        e = jnp.where(lane < 32, d0, jnp.where((lane >= 64) & (lane < 96), d1, eye))
+        e = jnp.concatenate(
+            block_inverse([e[8 * i : 8 * i + 8] for i in range(4)]), axis=0
+        )
+        inside = (col >= at) & (col < below)
+        wide_eye = jnp.where(col - at == wide_row, 1.0, 0.0)
+        panels, blocks = [], []
+        for m in range(2):
+            t = turned(e, 96 - 64 * m)[:, 0:32]
+            panel = exact_dot(t, jnp.where(inside, wide_eye, a_ref[m, at:below, :]))
+            panels.append(panel)
+            if below < 256:
+                near = panel[:, low : low + 128]
+                change = exact_dot(near, near, TN)
+                blocks.append(
+                    a_ref[m, below : below + 32, low : low + 128]
+                    - change[below - low : below - low + 32, :]
+                )
+            a_ref[m, at:below, :] = panel
+            out[m, at:below, :] = jnp.where(col <= at + wide_row, panel, 0.0)
+        after(k)
 
 
 def main_kernel(
     bw, bn, wb, nb,
     ow, on, fac, sq,
     bh, bl, vh, vl, part, full, swap, land, gram, cross, w_first, slices, zland, gathered,
-    wpart, wfull, wland, inverse, sq_x, sq_y,
+    wpart, wfull, wland, inverse, sq_land,
     send, recv,
 ):
     z = lax.axis_index("mp")
@@ -278,12 +291,12 @@
 
     sibling = plane(x, y, 1 - c)
     xs = [plane(x + d, y, c) for d in (1, 2, 3)]
-    xos = [plane(x + d, y, 1 - c) for d in (1, 2, 3)]
+    others = [(d, {"fsdp": (f + d) % 32}) for d in range(1, 32)]
     ys = [plane(x, y + d, c) for d in (1, 2, 3)]
     zs = [{"mp": (z + d) % 8} for d in range(1, 8)]
 
     barrier = pltpu.get_barrier_semaphore()
-    partners = [sibling] + xs + xos + ys + zs
+    partners = [device for _, device in others] + zs
     for device in partners:
         pl.semaphore_signal(barrier, inc=1, device_id=device, device_id_type=MESH)
 
@@ -459,15 +472,15 @@
                     h, p * 32 + m * 16 : p * 32 + m * 16 + 16, :
                 ]
 
-    for k in range(8):
-        factor_block(gram, k)
+    exchanges = []
+
+    def after_block(k):
         if k % 2:
+            done = inverse.at[c, :, pl.ds(32 * (k - 1), 64)]
+            exchanges.append(links.start(done, done, sibling))
             z_step()
-    full_row = lax.broadcasted_iota(jnp.int32, (256, 256), 0)
-    full_col = lax.broadcasted_iota(jnp.int32, (256, 256), 1)
-    for m in range(2):
-        inverse[c, m] = jnp.where(full_row >= full_col, gram[m], 0.0)
-    exchange = links.start(inverse.at[c], inverse.at[c], sibling)
+
+    invert_factor(gram, inverse.at[c], after_block)
     for chain in chains:
         for _ in chain:
             pass
@@ -496,28 +509,21 @@
         for h, squares in enumerate(factor_of(0, c, kind)):
             row = pl.ds(pl.multiple_of((2 * kind + c) * 2, 2) + h, 1)
             sq[row, :] = squares
-    exchange.wait_recv()
+    for copy in exchanges:
+        copy.wait_recv()
     for kind in range(2):
         for h, squares in enumerate(factor_of(1, 1 - c, kind)):
             row = pl.ds(pl.multiple_of((2 * kind + 1 - c) * 2, 2) + h, 1)
             sq[row, :] = squares
-    sq_x[0] = sq[...]
-    sends = [
-        links.start(sq_x.at[0], sq_x.at[d + 1], device)
-        for d, device in enumerate([sibling] + xs + xos)
-    ]
+    sq_land[0] = sq[...]
+    sends = [links.start(sq_land.at[0], sq_land.at[d], device) for d, device in others]
     ortho_half(c)
-    for copy in sends:
+    ortho_half(1 - c)
+    total = sq_land[0]
+    for (d, _), copy in zip(others, sends):
         copy.wait_recv()
-    total = sq_x[0]
-    for d in range(7):
-        total = total + sq_x[d + 1]
-    sq_y[0] = total
-    sends = [links.start(sq_y.at[0], sq_y.at[d + 1], ys[d]) for d in range(3)]
-    ortho_half(1 - c)
-    for copy in sends:
-        copy.wait_recv()
-    sq[...] = sq_y[0] + sq_y[1] + sq_y[2] + sq_y[3]
+        total = total + sq_land[d]
+    sq[...] = total
     links.finish()
 
 
@@ -548,7 +554,7 @@
     vmem = pl.BlockSpec(memory_space=pltpu.VMEM)
     bw = wide_momentum + wide_grad.astype(F32)
     bn = narrow_momentum + narrow_grad.astype(F32)
-    copies = 144
+    copies = 160
     ow, on, fac, sq = pl.pallas_call(
         main_kernel,
         out_shape=(
@@ -578,8 +584,7 @@
             pltpu.VMEM((8, 128, RANK), F32),
             pltpu.VMEM((2, 4, 128, RANK), F32),
             pltpu.VMEM((2, 2, RANK, RANK), F32),
-            pltpu.VMEM((8, 8, 128), F32),
-            pltpu.VMEM((4, 8, 128), F32),
+            pltpu.VMEM((32, 8, 128), F32),
             pltpu.SemaphoreType.DMA((copies,)),
             pltpu.SemaphoreType.DMA((copies,)),
         ],

time: 96.6 us -> 95.3 us (0.987)
  Pallas kernels: 92.5 us -> 91.2 us
    pallas_call x1, Pallas kernels: 88.4 us -> 87.1 us  [local(): pl.pallas_call(main_kernel, out_shape=(jax.ShapeDtypeStruct((2, WIDE, RAN...]
where the time goes in v5:
time: 95.3 us; the launch traced here: 95.2 us
  Pallas kernels  91.2 us (96%)
  other arithmetic  3.16 us (3%)
    pallas_call x1, Pallas kernels, local(): pl.pallas_call(main_kernel, out_shape=(jax.ShapeDtypeStruct((2, WIDE, RAN...  87.1 us
    pallas_call x1, Pallas kernels, local(): pl.pallas_call(last_kernel, grid=(2, steps), out_shape=(jax.ShapeDtypeStr...  4.1 us
    add x1, other arithmetic, local(): bw = wide_momentum + wide_grad.astype(F32)  2.15 us

profile of v5, /device:TPU:1, one launch (start us, length us, event | category | flops | bytes accessed | tf_op | source)
XLA Modules:
  0.0 95.2 jit_solution(4380422853440631283)
XLA Ops:
  0.6 1.0 %convert_add_fusion.1.bn = f32[2,128,256]{2,1,0:T(8,128)S(1)} fusion(f32[2,128,256]{2,1,0:T(8,128)} %param.9, bf16[2,128,256]{2,1,0:T(8,128)(2,1)} %param.10), kind=kLoop, calls=%fused_computation.1 | loop fusion | flops 131072 | bytes 655360 | tf_op jit(solution)/shard_map/add | solution.py:556
  1.6 0.0 copy-start
  1.7 0.0 copy-start.1
  1.7 2.2 %convert_add_fusion.bw = f32[2,1024,256]{2,1,0:T(8,128)S(1)} fusion(f32[2,1024,256]{2,1,0:T(8,128)} %param.6, bf16[2,1024,256]{2,1,0:T(8,128)(2,1)} %param.7), kind=kLoop, calls=%fused_computation | loop fusion | flops 1048576 | bytes 5242880 | tf_op jit(solution)/shard_map/add | solution.py:555
  3.8 0.0 copy-done
  3.8 0.0 copy-done.1
  3.8 87.1 %shard_map.109 = (f32[2,1024,256]{2,1,0:T(8,128)S(1)}, f32[2,128,256]{2,1,0:T(8,128)S(1)}, f32[4,256,256]{2,1,0:T(8,128)S(1)}, f32[8,128]{1,0:T(8,128)S(1)}) custom-call(f32[2,1024,256]{2,1,0:T(8,128)S(1)} %convert_add_fusion.bw, f32[2,128,256]{2,1,0:T(8,128)S(1)} %convert_add_fusion.1.bn, f32[2,256,256]{2,1,0:T(8,128)S(1)} %copy-done, ...), custom_call_target="tpu_custom_call" | custom-call | tf_op jit(solution)/shard_map/pallas_call | solution.py:558
  91.0 4.1 %shard_map.110 = (f32[2,1024,256]{2,1,0:T(8,128)}, f32[2,256,256]{2,1,0:T(8,128)}, bf16[2,1024,256]{2,1,0:T(8,128)(2,1)}, f32[2,128,256]{2,1,0:T(8,128)}, f32[2,...) custom-call(f32[2,1024,256]{2,1,0:T(8,128)S(1)} %convert_add_fusion.bw, f32[2,128,256]{2,1,0:T(8,128)S(1)} %convert_add_fusion.1.bn, ...), custom_call_target="tpu_custom_call" | custom-call | tf_op jit(solution)/shard_map/pallas_call | solution.py:605
Async XLA Ops:
  1.6 2.2 %copy-start = (f32[2,256,256]{2,1,0:T(8,128)S(1)}, f32[2,256,256]{2,1,0:T(8,128)}, u32[]{:S(2)}) copy-start(f32[2,256,256]{2,1,0:T(8,128)} %wb.1) | copy-start | bytes 1572868
  1.7 2.2 %copy-start.1 = (f32[2,256,256]{2,1,0:T(8,128)S(1)}, f32[2,256,256]{2,1,0:T(8,128)}, u32[]{:S(2)}) copy-start(f32[2,256,256]{2,1,0:T(8,128)} %nb.1) | copy-start | bytes 1572868

commit v6 on v5

--- a/solution.py
+++ b/solution.py
@@ -190,15 +190,11 @@
     b.wait_recv()
 
 
-def together(first, second, after):
+def together(*stages):
     done = object()
-    ended = False
-    while first or second:
-        first = [s for s in first if next(s, done) is not done]
-        if not first and not ended:
-            after()
-            ended = True
-        second = [s for s in second if next(s, done) is not done]
+    live = list(stages)
+    while live:
+        live = [s for s in live if next(s, done) is not done]
 
 
 def block_inverse(e):
@@ -276,7 +272,7 @@
 def main_kernel(
     bw, bn, wb, nb,
     ow, on, fac, sq,
-    bh, bl, vh, vl, part, full, swap, land, gram, cross, w_first, slices, zland, gathered,
+    bh, bl, vh, vl, part, full, swap, land, gram, cross, slices, zland, gathered,
     wpart, wfull, wland, inverse, sq_land,
     send, recv,
 ):
@@ -301,8 +297,6 @@
         pl.semaphore_signal(barrier, inc=1, device_id=device, device_id_type=MESH)
 
     links = Links(send, recv)
-    sets = ((0, 640), (640, 512))
-    wide_b = WIDE - 640
 
     def split_basis(cc):
         for kind, basis in enumerate((wb, nb)):
@@ -320,29 +314,22 @@
         part[0, rows, :] = raw[:, 0:128]
         part[1, rows, :] = raw[:, 128:256]
 
-    def raw_set(cc, i):
-        lo, n = ((0, 640), (640, wide_b))[i]
-        raw_rows_of(cc, 0, lo, n, bw[cc, lo : lo + n, :])
-
-        if i == 1:
-            raw_rows_of(cc, 1, WIDE, NARROW, bn[cc])
+    def raw_half(cc):
+        split_basis(cc)
+        raw_rows_of(cc, 0, 0, 512, bw[cc, 0:512, :])
+        raw_rows_of(cc, 0, 512, 512, bw[cc, 512:1024, :])
+        raw_rows_of(cc, 1, WIDE, NARROW, bn[cc])
 
     def half_rows(cc, start, n):
         return pl.ds(pl.multiple_of(cc * HALF + start, 8), n)
 
-    split_basis(1 - c)
-    raw_set(1 - c, 0)
+    raw_half(1 - c)
     pl.semaphore_wait(barrier, len(partners))
-    exchanges = []
-    for i, (start, n) in enumerate(sets):
-        if i == 1:
-            raw_set(1 - c, 1)
-        exchanges.append(
-            links.start(
-                part.at[:, half_rows(1 - c, start, n)], swap.at[:, pl.ds(start, n)], sibling
-            )
-        )
-    split_basis(c)
+    mine = half_rows(c, 0, HALF)
+    exchange = links.start(part.at[:, half_rows(1 - c, 0, HALF)], swap, sibling)
+    raw_half(c)
+    exchange.wait_recv()
+    part[:, mine, :] += swap[...]
 
     x_ring = dict(q=x, peers=xs)
     y_ring = dict(q=y, peers=ys)
@@ -356,31 +343,21 @@
 
     shares = []
 
-    def whole_sum(i, h):
-        start, n = sets[i]
-        big, small = n // 4, n // 16
+    big, small = HALF // 4, HALF // 16
+
+    def whole_sum(h):
         first, second = (x_ring, y_ring) if h == 0 else (y_ring, x_ring)
         yield from ring_reduce(
-            links, part, part, h, base + start, big, big // 2, land=land.at[i, h, 0], **first
+            links, part, part, h, base, big, big // 2, land=land.at[h, 0], **first
         )
         yield from direct_reduce(
-            links, part, full, h, base + start + first["q"] * big, small,
-            land=land.at[i, h, 1], **second
-        )
-        yield from gather_both(full, h, base + start, (big, small), first, second)
-        done = full.at[h, half_rows(c, start, n)]
+            links, part, full, h, base + first["q"] * big, small, land=land.at[h, 1], **second
+        )
+        yield from gather_both(full, h, base, (big, small), first, second)
+        done = full.at[h, mine]
         shares.append(links.start(done, done, sibling))
 
-    stages = []
-    for i, (start, n) in enumerate(sets):
-        raw_set(c, i)
-        exchanges[i].wait_recv()
-        rows = half_rows(c, start, n)
-        part[:, rows, :] += swap[:, start : start + n, :]
-        for h in range(2):
-            stage = whole_sum(i, h)
-            next(stage)
-            stages.append(stage)
+    together(whole_sum(0), whole_sum(1))
 
     def raw_rows(start, n):
         rows = pl.ds(pl.multiple_of(start, 8), n)
@@ -403,12 +380,7 @@
             bf16_dot(b_high, low, TN) + bf16_dot(bl[rows, :], high, TN)
         )
 
-    def first_set():
-        gram[0] = own_gram(0, 640)
-        w_first[...] = w_of(c, 0, 640)
-
-    together(stages[0:2], stages[2:4], after=first_set)
-    gram[0] += own_gram(640, wide_b)
+    gram[0] = own_gram(0, WIDE)
     gram[1] = own_gram(WIDE, NARROW)
 
     places = (x * 4 + y, y * 4 + x)
@@ -428,7 +400,7 @@
     def z_chain(i):
         return z_reduce_gather(links, wpart, wfull, wland, 64 * i, 64, z, zs[0], zs[6])
 
-    put_w(0, 0, w_first[...] + w_of(c, 640, wide_b))
+    put_w(0, 0, w_of(c, 0, WIDE))
     put_w(0, 1, w_of(c, WIDE, NARROW))
     chains = [z_chain(0)]
     next(chains[0])
@@ -463,7 +435,7 @@
         for stage in stages:
             next(stage, None)
         if i < 3:
-            links.finish(36)
+            links.finish(24)
         z_step()
     for h in range(2):
         for p in range(16):
@@ -554,7 +526,7 @@
     vmem = pl.BlockSpec(memory_space=pltpu.VMEM)
     bw = wide_momentum + wide_grad.astype(F32)
     bn = narrow_momentum + narrow_grad.astype(F32)
-    copies = 160
+    copies = 136
     ow, on, fac, sq = pl.pallas_call(
         main_kernel,
         out_shape=(
@@ -573,10 +545,9 @@
             pltpu.VMEM((2, 2 * HALF, 128), F32),
             pltpu.VMEM((2, 2 * HALF, 128), F32),
             pltpu.VMEM((2, HALF, 128), F32),
-            pltpu.VMEM((2, 2, 2, 4, 160, 128), F32),
+            pltpu.VMEM((2, 2, 4, 288, 128), F32),
             pltpu.VMEM((2, RANK, RANK), F32),
             pltpu.VMEM((RANK, RANK), F32),
-            pltpu.VMEM((COLS, RANK), F32),
             pltpu.VMEM((8, 8, 128), F32),
             pltpu.VMEM((7, 8, 128), F32),
             pltpu.VMEM((2, 512, 128), F32),

time: 95.3 us -> 97.7 us (1.025)
  Pallas kernels: 91.2 us -> 93.8 us
    pallas_call x1, Pallas kernels: 87.1 us -> 89.7 us  [local(): pl.pallas_call(main_kernel, out_shape=(jax.ShapeDtypeStruct((2, WIDE, RAN...]
where the time goes in v6:
time: 97.7 us; the launch traced here: 97.6 us
  Pallas kernels  93.8 us (96%)
  other arithmetic  3.16 us (3%)
    pallas_call x1, Pallas kernels, local(): pl.pallas_call(main_kernel, out_shape=(jax.ShapeDtypeStruct((2, WIDE, RAN...  89.7 us
    pallas_call x1, Pallas kernels, local(): pl.pallas_call(last_kernel, grid=(2, steps), out_shape=(jax.ShapeDtypeStr...  4.1 us
    add x1, other arithmetic, local(): bw = wide_momentum + wide_grad.astype(F32)  2.15 us

profile of v6, /device:TPU:1, one launch (start us, length us, event | category | flops | bytes accessed | tf_op | source)
XLA Modules:
  0.0 97.6 jit_solution(825965142262240597)
XLA Ops:
  0.6 1.0 %convert_add_fusion.1.bn = f32[2,128,256]{2,1,0:T(8,128)S(1)} fusion(f32[2,128,256]{2,1,0:T(8,128)} %param.9, bf16[2,128,256]{2,1,0:T(8,128)(2,1)} %param.10), kind=kLoop, calls=%fused_computation.1 | loop fusion | flops 131072 | bytes 655360 | tf_op jit(solution)/shard_map/add | solution.py:528
  1.6 0.0 copy-start
  1.7 0.0 copy-start.1
  1.7 2.2 %convert_add_fusion.bw = f32[2,1024,256]{2,1,0:T(8,128)S(1)} fusion(f32[2,1024,256]{2,1,0:T(8,128)} %param.6, bf16[2,1024,256]{2,1,0:T(8,128)(2,1)} %param.7), kind=kLoop, calls=%fused_computation | loop fusion | flops 1048576 | bytes 5242880 | tf_op jit(solution)/shard_map/add | solution.py:527
  3.8 0.0 copy-done
  3.8 0.0 copy-done.1
  3.8 89.7 %shard_map.109 = (f32[2,1024,256]{2,1,0:T(8,128)S(1)}, f32[2,128,256]{2,1,0:T(8,128)S(1)}, f32[4,256,256]{2,1,0:T(8,128)S(1)}, f32[8,128]{1,0:T(8,128)S(1)}) custom-call(f32[2,1024,256]{2,1,0:T(8,128)S(1)} %convert_add_fusion.bw, f32[2,128,256]{2,1,0:T(8,128)S(1)} %convert_add_fusion.1.bn, f32[2,256,256]{2,1,0:T(8,128)S(1)} %copy-done, ...), custom_call_target="tpu_custom_call" | custom-call | tf_op jit(solution)/shard_map/pallas_call | solution.py:530
  93.5 4.1 %shard_map.110 = (f32[2,1024,256]{2,1,0:T(8,128)}, f32[2,256,256]{2,1,0:T(8,128)}, bf16[2,1024,256]{2,1,0:T(8,128)(2,1)}, f32[2,128,256]{2,1,0:T(8,128)}, f32[2,...) custom-call(f32[2,1024,256]{2,1,0:T(8,128)S(1)} %convert_add_fusion.bw, f32[2,128,256]{2,1,0:T(8,128)S(1)} %convert_add_fusion.1.bn, ...), custom_call_target="tpu_custom_call" | custom-call | tf_op jit(solution)/shard_map/pallas_call | solution.py:576
Async XLA Ops:
  1.6 2.2 %copy-start = (f32[2,256,256]{2,1,0:T(8,128)S(1)}, f32[2,256,256]{2,1,0:T(8,128)}, u32[]{:S(2)}) copy-start(f32[2,256,256]{2,1,0:T(8,128)} %wb.1) | copy-start | bytes 1572868
  1.7 2.2 %copy-start.1 = (f32[2,256,256]{2,1,0:T(8,128)S(1)}, f32[2,256,256]{2,1,0:T(8,128)}, u32[]{:S(2)}) copy-start(f32[2,256,256]{2,1,0:T(8,128)} %nb.1) | copy-start | bytes 1572868

commit v7 on v5

--- a/solution.py
+++ b/solution.py
@@ -455,15 +455,16 @@
     next(chains[1])
     for copy in gram_sends:
         copy.wait_recv()
-    stages = [
-        gather_both(gathered, 0, 0, (128, 32), x_ring, y_ring),
-        gather_both(gathered, 1, 0, (128, 32), y_ring, x_ring),
-    ]
-    for i in range(4):
+    def gather_gram(h, first, second):
+        yield from direct_gather(links, gathered, h, first["q"] * 128, 32, **second)
+        yield from direct_gather(links, gathered, h, 0, 128, **first)
+
+    stages = [gather_gram(0, x_ring, y_ring), gather_gram(1, y_ring, x_ring)]
+    for i in range(3):
         for stage in stages:
             next(stage, None)
-        if i < 3:
-            links.finish(36)
+        if i < 2:
+            links.finish(48)
         z_step()
     for h in range(2):
         for p in range(16):
@@ -481,10 +482,6 @@
             z_step()
 
     invert_factor(gram, inverse.at[c], after_block)
-    for chain in chains:
-        for _ in chain:
-            pass
-
     def times_inverse(a, cc, kind):
         i_high, i_low = split(inverse[cc, kind])
         high, low = split(a)
@@ -505,10 +502,14 @@
         ow[cc] = times_inverse(raw_rows(start, WIDE), cc, 0)
         on[cc] = times_inverse(raw_rows(start + WIDE, NARROW), cc, 1)
 
+    for _ in chains[0]:
+        pass
     for kind in range(2):
         for h, squares in enumerate(factor_of(0, c, kind)):
             row = pl.ds(pl.multiple_of((2 * kind + c) * 2, 2) + h, 1)
             sq[row, :] = squares
+    for _ in chains[1]:
+        pass
     for copy in exchanges:
         copy.wait_recv()
     for kind in range(2):
@@ -532,18 +533,22 @@
 ):
     kinds = ((bw, ow, wmo, wbo, wup, D), (bn, on, nmo, nbo, nup, KVW))
 
-    @pl.when(pl.program_id(1) == 0)
+    which, step = pl.program_id(0), pl.program_id(1)
+
+    @pl.when(step == 0)
     def _():
         for kind in range(2):
-            factor = fac[kind, 0]
-            basis = factor * lax.rsqrt(sq[kind, 0] + 1e-6)
+            factor = fac[kind, which]
+            basis = factor * lax.rsqrt(sq[kind, which] + 1e-6)
             kinds[kind][3][0] = basis
             f_t[kind] = factor.astype(BF16).T
             b_high[kind], b_low[kind] = split(basis.T)
 
     for kind, (buffer, ortho, m_out, _, update, rows) in enumerate(kinds):
-        o_high, o_low = split(ortho[0])
-        m_out[0] = buffer[0] - 0.05 * bf16_dot(o_high, f_t[kind])
+        n = m_out.shape[1]
+        at = pl.ds(pl.multiple_of(step * n, n), n)
+        o_high, o_low = split(ortho[which, at, :])
+        m_out[0] = buffer[which, at, :] - 0.05 * bf16_dot(o_high, f_t[kind])
         product = bf16_dot(o_high, b_high[kind]) + (
             bf16_dot(o_high, b_low[kind]) + bf16_dot(o_low, b_high[kind])
         )
@@ -596,9 +601,6 @@
     def rows(n):
         return pl.BlockSpec((1, n, COLS), lambda m, i: (m, i, 0))
 
-    def whole(*lead):
-        return pl.BlockSpec(lead, lambda m, i: (0, m, 0, 0))
-
     basis_out = pl.BlockSpec((1, COLS, RANK), lambda m, i: (m, 0, 0))
     steps = 2
     w, n = WIDE // steps, NARROW // steps
@@ -614,9 +616,8 @@
             jax.ShapeDtypeStruct((2, NARROW, COLS), BF16),
         ),
         in_specs=[
-            rows(w), rows(n), rows(w), rows(n),
-            whole(2, 1, COLS, RANK), whole(2, 1, 1, RANK),
-        ],
+            vmem,
+        ] * 6,
         out_specs=[rows(w), basis_out, rows(w), rows(n), basis_out, rows(n)],
         scratch_shapes=[pltpu.VMEM((2, RANK, COLS), BF16)] * 3,
         compiler_params=pltpu.CompilerParams(vmem_limit_bytes=24 * 2**20),

time: 95.3 us -> 95.6 us (level)
  no operation moved by 1% of the time
where the time goes in v7:
time: 95.6 us; the launch traced here: 95.5 us
  Pallas kernels  91.6 us (96%)
  other arithmetic  3.16 us (3%)
    pallas_call x1, Pallas kernels, local(): pl.pallas_call(main_kernel, out_shape=(jax.ShapeDtypeStruct((2, WIDE, RAN...  87.6 us
    pallas_call x1, Pallas kernels, local(): pl.pallas_call(last_kernel, grid=(2, steps), out_shape=(jax.ShapeDtypeStr...  4.02 us
    add x1, other arithmetic, local(): bw = wide_momentum + wide_grad.astype(F32)  2.15 us

profile of v7, /device:TPU:1, one launch (start us, length us, event | category | flops | bytes accessed | tf_op | source)
XLA Modules:
  0.0 95.5 jit_solution(10636692368480272968)
XLA Ops:
  0.6 1.0 %convert_add_fusion.1.bn = f32[2,128,256]{2,1,0:T(8,128)S(1)} fusion(f32[2,128,256]{2,1,0:T(8,128)} %param.9, bf16[2,128,256]{2,1,0:T(8,128)(2,1)} %param.10), kind=kLoop, calls=%fused_computation.1 | loop fusion | flops 131072 | bytes 655360 | tf_op jit(solution)/shard_map/add | solution.py:561
  1.6 0.0 copy-start
  1.7 0.0 copy-start.1
  1.7 2.2 %convert_add_fusion.bw = f32[2,1024,256]{2,1,0:T(8,128)S(1)} fusion(f32[2,1024,256]{2,1,0:T(8,128)} %param.6, bf16[2,1024,256]{2,1,0:T(8,128)(2,1)} %param.7), kind=kLoop, calls=%fused_computation | loop fusion | flops 1048576 | bytes 5242880 | tf_op jit(solution)/shard_map/add | solution.py:560
  3.8 0.0 copy-done
  3.8 0.0 copy-done.1
  3.8 87.6 %shard_map.109 = (f32[2,1024,256]{2,1,0:T(8,128)S(1)}, f32[2,128,256]{2,1,0:T(8,128)S(1)}, f32[4,256,256]{2,1,0:T(8,128)S(1)}, f32[8,128]{1,0:T(8,128)S(1)}) custom-call(f32[2,1024,256]{2,1,0:T(8,128)S(1)} %convert_add_fusion.bw, f32[2,128,256]{2,1,0:T(8,128)S(1)} %convert_add_fusion.1.bn, f32[2,256,256]{2,1,0:T(8,128)S(1)} %copy-done, ...), custom_call_target="tpu_custom_call" | custom-call | tf_op jit(solution)/shard_map/pallas_call | solution.py:563
  91.5 4.0 %shard_map.110 = (f32[2,1024,256]{2,1,0:T(8,128)}, f32[2,256,256]{2,1,0:T(8,128)}, bf16[2,1024,256]{2,1,0:T(8,128)(2,1)}, f32[2,128,256]{2,1,0:T(8,128)}, f32[2,...) custom-call(f32[2,1024,256]{2,1,0:T(8,128)S(1)} %convert_add_fusion.bw, f32[2,128,256]{2,1,0:T(8,128)S(1)} %convert_add_fusion.1.bn, ...), custom_call_target="tpu_custom_call" | custom-call | tf_op jit(solution)/shard_map/pallas_call | solution.py:607
Async XLA Ops:
  1.6 2.2 %copy-start = (f32[2,256,256]{2,1,0:T(8,128)S(1)}, f32[2,256,256]{2,1,0:T(8,128)}, u32[]{:S(2)}) copy-start(f32[2,256,256]{2,1,0:T(8,128)} %wb.1) | copy-start | bytes 1572868
  1.7 2.2 %copy-start.1 = (f32[2,256,256]{2,1,0:T(8,128)S(1)}, f32[2,256,256]{2,1,0:T(8,128)}, u32[]{:S(2)}) copy-start(f32[2,256,256]{2,1,0:T(8,128)} %nb.1) | copy-start | bytes 1572868

commit v8 on v7

--- a/solution.py
+++ b/solution.py
@@ -408,6 +408,19 @@
         w_first[...] = w_of(c, 0, 640)
 
     together(stages[0:2], stages[2:4], after=first_set)
+    def put_w(i, kind, w):
+        row = i * 64 + kind * 32
+        for k in range(8):
+            wpart[k, row : row + 32, :] = w[k * 32 : k * 32 + 32, :]
+
+    def z_chain(i):
+        return z_reduce_gather(links, wpart, wfull, wland, 64 * i, 64, z, zs[0], zs[6])
+
+    put_w(0, 0, w_first[...] + w_of(c, 640, wide_b))
+    put_w(0, 1, w_of(c, WIDE, NARROW))
+    chains = [z_chain(0)]
+    next(chains[0])
+
     gram[0] += own_gram(640, wide_b)
     gram[1] = own_gram(WIDE, NARROW)
 
@@ -420,18 +433,12 @@
         links.start(slices.at[(z + d) % 8], zland.at[d - 1], zs[d - 1]) for d in range(1, 8)
     ]
 
-    def put_w(i, kind, w):
-        row = i * 64 + kind * 32
-        for k in range(8):
-            wpart[k, row : row + 32, :] = w[k * 32 : k * 32 + 32, :]
-
-    def z_chain(i):
-        return z_reduce_gather(links, wpart, wfull, wland, 64 * i, 64, z, zs[0], zs[6])
-
-    put_w(0, 0, w_first[...] + w_of(c, 640, wide_b))
-    put_w(0, 1, w_of(c, WIDE, NARROW))
-    chains = [z_chain(0)]
-    next(chains[0])
+    for copy in shares:
+        copy.wait_recv()
+    put_w(1, 0, w_of(1 - c, 0, WIDE))
+    put_w(1, 1, w_of(1 - c, WIDE, NARROW))
+    chains.append(z_chain(1))
+    next(chains[1])
 
     def z_step():
         for chain in chains:
@@ -446,13 +453,7 @@
     own = gathered.at[z // 4, pl.ds(pl.multiple_of(place * 32 + (z % 4) * 8, 8), 8)]
     own[...] = total
     gram_sends = [links.start(own, own, zs[d]) for d in range(7)]
-    for copy in shares:
-        copy.wait_recv()
-    put_w(1, 0, w_of(1 - c, 0, WIDE))
-    put_w(1, 1, w_of(1 - c, WIDE, NARROW))
     z_step()
-    chains.append(z_chain(1))
-    next(chains[1])
     for copy in gram_sends:
         copy.wait_recv()
     def gather_gram(h, first, second):

time: 95.6 us -> 92.7 us (0.970)
  Pallas kernels: 91.6 us -> 88.7 us
    pallas_call x1, Pallas kernels: 87.6 us -> 84.7 us  [local(): pl.pallas_call(main_kernel, out_shape=(jax.ShapeDtypeStruct((2, WIDE, RAN...]
where the time goes in v8:
time: 92.7 us; the launch traced here: 92.5 us
  Pallas kernels  88.7 us (96%)
  other arithmetic  3.16 us (3%)
    pallas_call x1, Pallas kernels, local(): pl.pallas_call(main_kernel, out_shape=(jax.ShapeDtypeStruct((2, WIDE, RAN...  84.7 us
    pallas_call x1, Pallas kernels, local(): pl.pallas_call(last_kernel, grid=(2, steps), out_shape=(jax.ShapeDtypeStr...  4.02 us
    add x1, other arithmetic, local(): bw = wide_momentum + wide_grad.astype(F32)  2.15 us

profile of v8, /device:TPU:1, one launch (start us, length us, event | category | flops | bytes accessed | tf_op | source)
XLA Modules:
  0.0 92.5 jit_solution(14314774683622718603)
XLA Ops:
  0.6 1.0 %convert_add_fusion.1.bn = f32[2,128,256]{2,1,0:T(8,128)S(1)} fusion(f32[2,128,256]{2,1,0:T(8,128)} %param.9, bf16[2,128,256]{2,1,0:T(8,128)(2,1)} %param.10), kind=kLoop, calls=%fused_computation.1 | loop fusion | flops 131072 | bytes 655360 | tf_op jit(solution)/shard_map/add | solution.py:562
  1.6 0.0 copy-start
  1.7 0.0 copy-start.1
  1.7 2.2 %convert_add_fusion.bw = f32[2,1024,256]{2,1,0:T(8,128)S(1)} fusion(f32[2,1024,256]{2,1,0:T(8,128)} %param.6, bf16[2,1024,256]{2,1,0:T(8,128)(2,1)} %param.7), kind=kLoop, calls=%fused_computation | loop fusion | flops 1048576 | bytes 5242880 | tf_op jit(solution)/shard_map/add | solution.py:561
  3.8 0.0 copy-done
  3.8 0.0 copy-done.1
  3.8 84.7 %shard_map.109 = (f32[2,1024,256]{2,1,0:T(8,128)S(1)}, f32[2,128,256]{2,1,0:T(8,128)S(1)}, f32[4,256,256]{2,1,0:T(8,128)S(1)}, f32[8,128]{1,0:T(8,128)S(1)}) custom-call(f32[2,1024,256]{2,1,0:T(8,128)S(1)} %convert_add_fusion.bw, f32[2,128,256]{2,1,0:T(8,128)S(1)} %convert_add_fusion.1.bn, f32[2,256,256]{2,1,0:T(8,128)S(1)} %copy-done, ...), custom_call_target="tpu_custom_call" | custom-call | tf_op jit(solution)/shard_map/pallas_call | solution.py:564
  88.5 4.0 %shard_map.110 = (f32[2,1024,256]{2,1,0:T(8,128)}, f32[2,256,256]{2,1,0:T(8,128)}, bf16[2,1024,256]{2,1,0:T(8,128)(2,1)}, f32[2,128,256]{2,1,0:T(8,128)}, f32[2,...) custom-call(f32[2,1024,256]{2,1,0:T(8,128)S(1)} %convert_add_fusion.bw, f32[2,128,256]{2,1,0:T(8,128)S(1)} %convert_add_fusion.1.bn, ...), custom_call_target="tpu_custom_call" | custom-call | tf_op jit(solution)/shard_map/pallas_call | solution.py:608
Async XLA Ops:
  1.6 2.2 %copy-start = (f32[2,256,256]{2,1,0:T(8,128)S(1)}, f32[2,256,256]{2,1,0:T(8,128)}, u32[]{:S(2)}) copy-start(f32[2,256,256]{2,1,0:T(8,128)} %wb.1) | copy-start | bytes 1572868
  1.7 2.2 %copy-start.1 = (f32[2,256,256]{2,1,0:T(8,128)S(1)}, f32[2,256,256]{2,1,0:T(8,128)}, u32[]{:S(2)}) copy-start(f32[2,256,256]{2,1,0:T(8,128)} %nb.1) | copy-start | bytes 1572868

commit v9 on v8

--- a/solution.py
+++ b/solution.py
@@ -413,13 +413,17 @@
         for k in range(8):
             wpart[k, row : row + 32, :] = w[k * 32 : k * 32 + 32, :]
 
-    def z_chain(i):
-        return z_reduce_gather(links, wpart, wfull, wland, 64 * i, 64, z, zs[0], zs[6])
-
-    put_w(0, 0, w_first[...] + w_of(c, 640, wide_b))
-    put_w(0, 1, w_of(c, WIDE, NARROW))
-    chains = [z_chain(0)]
-    next(chains[0])
+    chains = []
+
+    def z_chain(i, kind, w):
+        put_w(i, kind, w)
+        row = i * 64 + kind * 32
+        chain = z_reduce_gather(links, wpart, wfull, wland, row, 32, z, zs[0], zs[6])
+        next(chain)
+        chains.append(chain)
+
+    z_chain(0, 0, w_first[...] + w_of(c, 640, wide_b))
+    z_chain(0, 1, w_of(c, WIDE, NARROW))
 
     gram[0] += own_gram(640, wide_b)
     gram[1] = own_gram(WIDE, NARROW)
@@ -435,10 +439,8 @@
 
     for copy in shares:
         copy.wait_recv()
-    put_w(1, 0, w_of(1 - c, 0, WIDE))
-    put_w(1, 1, w_of(1 - c, WIDE, NARROW))
-    chains.append(z_chain(1))
-    next(chains[1])
+    z_chain(1, 0, w_of(1 - c, 0, WIDE))
+    z_chain(1, 1, w_of(1 - c, WIDE, NARROW))
 
     def z_step():
         for chain in chains:
@@ -465,7 +467,7 @@
         for stage in stages:
             next(stage, None)
         if i < 2:
-            links.finish(48)
+            links.finish(40)
         z_step()
     for h in range(2):
         for p in range(16):
@@ -503,14 +505,16 @@
         ow[cc] = times_inverse(raw_rows(start, WIDE), cc, 0)
         on[cc] = times_inverse(raw_rows(start + WIDE, NARROW), cc, 1)
 
-    for _ in chains[0]:
-        pass
+    for chain in chains[0:2]:
+        for _ in chain:
+            pass
     for kind in range(2):
         for h, squares in enumerate(factor_of(0, c, kind)):
             row = pl.ds(pl.multiple_of((2 * kind + c) * 2, 2) + h, 1)
             sq[row, :] = squares
-    for _ in chains[1]:
-        pass
+    for chain in chains[2:4]:
+        for _ in chain:
+            pass
     for copy in exchanges:
         copy.wait_recv()
     for kind in range(2):
@@ -560,7 +564,7 @@
     vmem = pl.BlockSpec(memory_space=pltpu.VMEM)
     bw = wide_momentum + wide_grad.astype(F32)
     bn = narrow_momentum + narrow_grad.astype(F32)
-    copies = 160
+    copies = 192
     ow, on, fac, sq = pl.pallas_call(
         main_kernel,
         out_shape=(

time: 92.7 us -> 91.2 us (0.984)
  Pallas kernels: 88.7 us -> 87.2 us
    pallas_call x1, Pallas kernels: 84.7 us -> 83.2 us  [local(): pl.pallas_call(main_kernel, out_shape=(jax.ShapeDtypeStruct((2, WIDE, RAN...]
where the time goes in v9:
time: 91.2 us; the launch traced here: 91.1 us
  Pallas kernels  87.2 us (96%)
  other arithmetic  3.16 us (3%)
    pallas_call x1, Pallas kernels, local(): pl.pallas_call(main_kernel, out_shape=(jax.ShapeDtypeStruct((2, WIDE, RAN...  83.2 us
    pallas_call x1, Pallas kernels, local(): pl.pallas_call(last_kernel, grid=(2, steps), out_shape=(jax.ShapeDtypeStr...  4.02 us
    add x1, other arithmetic, local(): bw = wide_momentum + wide_grad.astype(F32)  2.15 us

profile of v9, /device:TPU:1, one launch (start us, length us, event | category | flops | bytes accessed | tf_op | source)
XLA Modules:
  0.0 91.1 jit_solution(8030403656427330087)
XLA Ops:
  0.6 1.0 %convert_add_fusion.1.bn = f32[2,128,256]{2,1,0:T(8,128)S(1)} fusion(f32[2,128,256]{2,1,0:T(8,128)} %param.9, bf16[2,128,256]{2,1,0:T(8,128)(2,1)} %param.10), kind=kLoop, calls=%fused_computation.1 | loop fusion | flops 131072 | bytes 655360 | tf_op jit(solution)/shard_map/add | solution.py:566
  1.6 0.0 copy-start
  1.7 0.0 copy-start.1
  1.7 2.2 %convert_add_fusion.bw = f32[2,1024,256]{2,1,0:T(8,128)S(1)} fusion(f32[2,1024,256]{2,1,0:T(8,128)} %param.6, bf16[2,1024,256]{2,1,0:T(8,128)(2,1)} %param.7), kind=kLoop, calls=%fused_computation | loop fusion | flops 1048576 | bytes 5242880 | tf_op jit(solution)/shard_map/add | solution.py:565
  3.8 0.0 copy-done
  3.8 0.0 copy-done.1
  3.8 83.2 %shard_map.109 = (f32[2,1024,256]{2,1,0:T(8,128)S(1)}, f32[2,128,256]{2,1,0:T(8,128)S(1)}, f32[4,256,256]{2,1,0:T(8,128)S(1)}, f32[8,128]{1,0:T(8,128)S(1)}) custom-call(f32[2,1024,256]{2,1,0:T(8,128)S(1)} %convert_add_fusion.bw, f32[2,128,256]{2,1,0:T(8,128)S(1)} %convert_add_fusion.1.bn, f32[2,256,256]{2,1,0:T(8,128)S(1)} %copy-done, ...), custom_call_target="tpu_custom_call" | custom-call | tf_op jit(solution)/shard_map/pallas_call | solution.py:568
  87.0 4.0 %shard_map.110 = (f32[2,1024,256]{2,1,0:T(8,128)}, f32[2,256,256]{2,1,0:T(8,128)}, bf16[2,1024,256]{2,1,0:T(8,128)(2,1)}, f32[2,128,256]{2,1,0:T(8,128)}, f32[2,...) custom-call(f32[2,1024,256]{2,1,0:T(8,128)S(1)} %convert_add_fusion.bw, f32[2,128,256]{2,1,0:T(8,128)S(1)} %convert_add_fusion.1.bn, ...), custom_call_target="tpu_custom_call" | custom-call | tf_op jit(solution)/shard_map/pallas_call | solution.py:612
Async XLA Ops:
  1.6 2.2 %copy-start = (f32[2,256,256]{2,1,0:T(8,128)S(1)}, f32[2,256,256]{2,1,0:T(8,128)}, u32[]{:S(2)}) copy-start(f32[2,256,256]{2,1,0:T(8,128)} %wb.1) | copy-start | bytes 1572868
  1.7 2.2 %copy-start.1 = (f32[2,256,256]{2,1,0:T(8,128)S(1)}, f32[2,256,256]{2,1,0:T(8,128)}, u32[]{:S(2)}) copy-start(f32[2,256,256]{2,1,0:T(8,128)} %nb.1) | copy-start | bytes 1572868

commit v10 on v9

--- a/solution.py
+++ b/solution.py
@@ -442,8 +442,9 @@
     z_chain(1, 0, w_of(1 - c, 0, WIDE))
     z_chain(1, 1, w_of(1 - c, WIDE, NARROW))
 
-    def z_step():
-        for chain in chains:
+    def z_step(live=4, sent=0):
+        links.finish(sent)
+        for chain in chains[0:live]:
             next(chain, None)
 
     for copy in gram_sends:
@@ -455,7 +456,7 @@
     own = gathered.at[z // 4, pl.ds(pl.multiple_of(place * 32 + (z % 4) * 8, 8), 8)]
     own[...] = total
     gram_sends = [links.start(own, own, zs[d]) for d in range(7)]
-    z_step()
+    z_step(live=2)
     for copy in gram_sends:
         copy.wait_recv()
     def gather_gram(h, first, second):
@@ -482,7 +483,8 @@
         if k % 2:
             done = inverse.at[c, :, pl.ds(32 * (k - 1), 64)]
             exchanges.append(links.start(done, done, sibling))
-            z_step()
+        if k in (1, 3, 4, 6, 7):
+            z_step(sent=16)
 
     invert_factor(gram, inverse.at[c], after_block)
     def times_inverse(a, cc, kind):

time: 91.2 us -> 94.8 us (1.039)
  Pallas kernels: 87.2 us -> 90.8 us
    pallas_call x1, Pallas kernels: 83.2 us -> 86.8 us  [local(): pl.pallas_call(main_kernel, out_shape=(jax.ShapeDtypeStruct((2, WIDE, RAN...]
where the time goes in v10:
time: 94.8 us; the launch traced here: 94.7 us
  Pallas kernels  90.8 us (96%)
  other arithmetic  3.16 us (3%)
    pallas_call x1, Pallas kernels, local(): pl.pallas_call(main_kernel, out_shape=(jax.ShapeDtypeStruct((2, WIDE, RAN...  86.8 us
    pallas_call x1, Pallas kernels, local(): pl.pallas_call(last_kernel, grid=(2, steps), out_shape=(jax.ShapeDtypeStr...  4.02 us
    add x1, other arithmetic, local(): bw = wide_momentum + wide_grad.astype(F32)  2.15 us

profile of v10, /device:TPU:1, one launch (start us, length us, event | category | flops | bytes accessed | tf_op | source)
XLA Modules:
  0.0 94.7 jit_solution(385736623657852995)
XLA Ops:
  0.6 1.0 %convert_add_fusion.1.bn = f32[2,128,256]{2,1,0:T(8,128)S(1)} fusion(f32[2,128,256]{2,1,0:T(8,128)} %param.9, bf16[2,128,256]{2,1,0:T(8,128)(2,1)} %param.10), kind=kLoop, calls=%fused_computation.1 | loop fusion | flops 131072 | bytes 655360 | tf_op jit(solution)/shard_map/add | solution.py:568
  1.6 0.0 copy-start
  1.7 0.0 copy-start.1
  1.7 2.2 %convert_add_fusion.bw = f32[2,1024,256]{2,1,0:T(8,128)S(1)} fusion(f32[2,1024,256]{2,1,0:T(8,128)} %param.6, bf16[2,1024,256]{2,1,0:T(8,128)(2,1)} %param.7), kind=kLoop, calls=%fused_computation | loop fusion | flops 1048576 | bytes 5242880 | tf_op jit(solution)/shard_map/add | solution.py:567
  3.8 0.0 copy-done
  3.8 0.0 copy-done.1
  3.8 86.8 %shard_map.109 = (f32[2,1024,256]{2,1,0:T(8,128)S(1)}, f32[2,128,256]{2,1,0:T(8,128)S(1)}, f32[4,256,256]{2,1,0:T(8,128)S(1)}, f32[8,128]{1,0:T(8,128)S(1)}) custom-call(f32[2,1024,256]{2,1,0:T(8,128)S(1)} %convert_add_fusion.bw, f32[2,128,256]{2,1,0:T(8,128)S(1)} %convert_add_fusion.1.bn, f32[2,256,256]{2,1,0:T(8,128)S(1)} %copy-done, ...), custom_call_target="tpu_custom_call" | custom-call | tf_op jit(solution)/shard_map/pallas_call | solution.py:570
  90.7 4.0 %shard_map.110 = (f32[2,1024,256]{2,1,0:T(8,128)}, f32[2,256,256]{2,1,0:T(8,128)}, bf16[2,1024,256]{2,1,0:T(8,128)(2,1)}, f32[2,128,256]{2,1,0:T(8,128)}, f32[2,...) custom-call(f32[2,1024,256]{2,1,0:T(8,128)S(1)} %convert_add_fusion.bw, f32[2,128,256]{2,1,0:T(8,128)S(1)} %convert_add_fusion.1.bn, ...), custom_call_target="tpu_custom_call" | custom-call | tf_op jit(solution)/shard_map/pallas_call | solution.py:614
Async XLA Ops:
  1.6 2.2 %copy-start = (f32[2,256,256]{2,1,0:T(8,128)S(1)}, f32[2,256,256]{2,1,0:T(8,128)}, u32[]{:S(2)}) copy-start(f32[2,256,256]{2,1,0:T(8,128)} %wb.1) | copy-start | bytes 1572868
  1.7 2.2 %copy-start.1 = (f32[2,256,256]{2,1,0:T(8,128)S(1)}, f32[2,256,256]{2,1,0:T(8,128)}, u32[]{:S(2)}) copy-start(f32[2,256,256]{2,1,0:T(8,128)} %nb.1) | copy-start | bytes 1572868

commit v11 on v10

--- a/solution.py
+++ b/solution.py
@@ -442,8 +442,7 @@
     z_chain(1, 0, w_of(1 - c, 0, WIDE))
     z_chain(1, 1, w_of(1 - c, WIDE, NARROW))
 
-    def z_step(live=4, sent=0):
-        links.finish(sent)
+    def z_step(live=4):
         for chain in chains[0:live]:
             next(chain, None)
 
@@ -483,8 +482,7 @@
         if k % 2:
             done = inverse.at[c, :, pl.ds(32 * (k - 1), 64)]
             exchanges.append(links.start(done, done, sibling))
-        if k in (1, 3, 4, 6, 7):
-            z_step(sent=16)
+            z_step()
 
     invert_factor(gram, inverse.at[c], after_block)
     def times_inverse(a, cc, kind):
@@ -514,6 +512,7 @@
         for h, squares in enumerate(factor_of(0, c, kind)):
             row = pl.ds(pl.multiple_of((2 * kind + c) * 2, 2) + h, 1)
             sq[row, :] = squares
+    links.finish(40)
     for chain in chains[2:4]:
         for _ in chain:
             pass
@@ -609,7 +608,7 @@
         return pl.BlockSpec((1, n, COLS), lambda m, i: (m, i, 0))
 
     basis_out = pl.BlockSpec((1, COLS, RANK), lambda m, i: (m, 0, 0))
-    steps = 2
+    steps = 4
     w, n = WIDE // steps, NARROW // steps
     return pl.pallas_call(
         last_kernel,

time: 94.8 us -> 95.3 us (level)
    pallas_call x1, Pallas kernels: 4.02 us -> 5.34 us  [local(): pl.pallas_call(last_kernel, grid=(2, steps), out_shape=(jax.ShapeDtypeStr...]
where the time goes in v11:
time: 95.3 us; the launch traced here: 95.2 us
  Pallas kernels  91.3 us (96%)
  other arithmetic  3.16 us (3%)
    pallas_call x1, Pallas kernels, local(): pl.pallas_call(main_kernel, out_shape=(jax.ShapeDtypeStruct((2, WIDE, RAN...  85.9 us
    pallas_call x1, Pallas kernels, local(): pl.pallas_call(last_kernel, grid=(2, steps), out_shape=(jax.ShapeDtypeStr...  5.34 us
    add x1, other arithmetic, local(): bw = wide_momentum + wide_grad.astype(F32)  2.15 us

profile of v11, /device:TPU:1, one launch (start us, length us, event | category | flops | bytes accessed | tf_op | source)
XLA Modules:
  0.0 95.2 jit_solution(1796631551762241980)
XLA Ops:
  0.6 1.0 %convert_add_fusion.1.bn = f32[2,128,256]{2,1,0:T(8,128)S(1)} fusion(f32[2,128,256]{2,1,0:T(8,128)} %param.9, bf16[2,128,256]{2,1,0:T(8,128)(2,1)} %param.10), kind=kLoop, calls=%fused_computation.1 | loop fusion | flops 131072 | bytes 655360 | tf_op jit(solution)/shard_map/add | solution.py:567
  1.6 0.0 copy-start
  1.7 0.0 copy-start.1
  1.7 2.2 %convert_add_fusion.bw = f32[2,1024,256]{2,1,0:T(8,128)S(1)} fusion(f32[2,1024,256]{2,1,0:T(8,128)} %param.6, bf16[2,1024,256]{2,1,0:T(8,128)(2,1)} %param.7), kind=kLoop, calls=%fused_computation | loop fusion | flops 1048576 | bytes 5242880 | tf_op jit(solution)/shard_map/add | solution.py:566
  3.8 0.0 copy-done
  3.8 0.0 copy-done.1
  3.8 85.9 %shard_map.109 = (f32[2,1024,256]{2,1,0:T(8,128)S(1)}, f32[2,128,256]{2,1,0:T(8,128)S(1)}, f32[4,256,256]{2,1,0:T(8,128)S(1)}, f32[8,128]{1,0:T(8,128)S(1)}) custom-call(f32[2,1024,256]{2,1,0:T(8,128)S(1)} %convert_add_fusion.bw, f32[2,128,256]{2,1,0:T(8,128)S(1)} %convert_add_fusion.1.bn, f32[2,256,256]{2,1,0:T(8,128)S(1)} %copy-done, ...), custom_call_target="tpu_custom_call" | custom-call | tf_op jit(solution)/shard_map/pallas_call | solution.py:569
  89.8 5.3 %shard_map.110 = (f32[2,1024,256]{2,1,0:T(8,128)}, f32[2,256,256]{2,1,0:T(8,128)}, bf16[2,1024,256]{2,1,0:T(8,128)(2,1)}, f32[2,128,256]{2,1,0:T(8,128)}, f32[2,...) custom-call(f32[2,1024,256]{2,1,0:T(8,128)S(1)} %convert_add_fusion.bw, f32[2,128,256]{2,1,0:T(8,128)S(1)} %convert_add_fusion.1.bn, ...), custom_call_target="tpu_custom_call" | custom-call | tf_op jit(solution)/shard_map/pallas_call | solution.py:613
Async XLA Ops:
  1.6 2.2 %copy-start = (f32[2,256,256]{2,1,0:T(8,128)S(1)}, f32[2,256,256]{2,1,0:T(8,128)}, u32[]{:S(2)}) copy-start(f32[2,256,256]{2,1,0:T(8,128)} %wb.1) | copy-start | bytes 1572868
  1.7 2.2 %copy-start.1 = (f32[2,256,256]{2,1,0:T(8,128)S(1)}, f32[2,256,256]{2,1,0:T(8,128)}, u32[]{:S(2)}) copy-start(f32[2,256,256]{2,1,0:T(8,128)} %nb.1) | copy-start | bytes 1572868

commit v12 on v9

--- a/solution.py
+++ b/solution.py
@@ -482,6 +482,7 @@
         if k % 2:
             done = inverse.at[c, :, pl.ds(32 * (k - 1), 64)]
             exchanges.append(links.start(done, done, sibling))
+        else:
             z_step()
 
     invert_factor(gram, inverse.at[c], after_block)
@@ -607,7 +608,7 @@
         return pl.BlockSpec((1, n, COLS), lambda m, i: (m, i, 0))
 
     basis_out = pl.BlockSpec((1, COLS, RANK), lambda m, i: (m, 0, 0))
-    steps = 2
+    steps = 1
     w, n = WIDE // steps, NARROW // steps
     return pl.pallas_call(
         last_kernel,

time: 91.2 us -> 91.6 us (level)
    pallas_call x1, Pallas kernels: 83.2 us -> 84.4 us  [local(): pl.pallas_call(main_kernel, out_shape=(jax.ShapeDtypeStruct((2, WIDE, RAN...]
where the time goes in v12:
time: 91.6 us; the launch traced here: 91.5 us
  Pallas kernels  87.6 us (96%)
  other arithmetic  3.16 us (3%)
    pallas_call x1, Pallas kernels, local(): pl.pallas_call(main_kernel, out_shape=(jax.ShapeDtypeStruct((2, WIDE, RAN...  84.4 us
    pallas_call x1, Pallas kernels, local(): pl.pallas_call(last_kernel, grid=(2, steps), out_shape=(jax.ShapeDtypeStr...  3.2 us
    add x1, other arithmetic, local(): bw = wide_momentum + wide_grad.astype(F32)  2.15 us

profile of v12, /device:TPU:1, one launch (start us, length us, event | category | flops | bytes accessed | tf_op | source)
XLA Modules:
  0.0 91.5 jit_solution(6915788298575127679)
XLA Ops:
  0.6 1.0 %convert_add_fusion.1.bn = f32[2,128,256]{2,1,0:T(8,128)S(1)} fusion(f32[2,128,256]{2,1,0:T(8,128)} %param.9, bf16[2,128,256]{2,1,0:T(8,128)(2,1)} %param.10), kind=kLoop, calls=%fused_computation.1 | loop fusion | flops 131072 | bytes 655360 | tf_op jit(solution)/shard_map/add | solution.py:567
  1.6 0.0 copy-start
  1.7 0.0 copy-start.1
  1.7 2.2 %convert_add_fusion.bw = f32[2,1024,256]{2,1,0:T(8,128)S(1)} fusion(f32[2,1024,256]{2,1,0:T(8,128)} %param.6, bf16[2,1024,256]{2,1,0:T(8,128)(2,1)} %param.7), kind=kLoop, calls=%fused_computation | loop fusion | flops 1048576 | bytes 5242880 | tf_op jit(solution)/shard_map/add | solution.py:566
  3.8 0.0 copy-done
  3.8 0.0 copy-done.1
  3.8 84.4 %shard_map.109 = (f32[2,1024,256]{2,1,0:T(8,128)S(1)}, f32[2,128,256]{2,1,0:T(8,128)S(1)}, f32[4,256,256]{2,1,0:T(8,128)S(1)}, f32[8,128]{1,0:T(8,128)S(1)}) custom-call(f32[2,1024,256]{2,1,0:T(8,128)S(1)} %convert_add_fusion.bw, f32[2,128,256]{2,1,0:T(8,128)S(1)} %convert_add_fusion.1.bn, f32[2,256,256]{2,1,0:T(8,128)S(1)} %copy-done, ...), custom_call_target="tpu_custom_call" | custom-call | tf_op jit(solution)/shard_map/pallas_call | solution.py:569
  88.3 3.2 %shard_map.110 = (f32[2,1024,256]{2,1,0:T(8,128)}, f32[2,256,256]{2,1,0:T(8,128)}, bf16[2,1024,256]{2,1,0:T(8,128)(2,1)}, f32[2,128,256]{2,1,0:T(8,128)}, f32[2,...) custom-call(f32[2,1024,256]{2,1,0:T(8,128)S(1)} %convert_add_fusion.bw, f32[2,128,256]{2,1,0:T(8,128)S(1)} %convert_add_fusion.1.bn, ...), custom_call_target="tpu_custom_call" | custom-call | tf_op jit(solution)/shard_map/pallas_call | solution.py:613
Async XLA Ops:
  1.6 2.2 %copy-start = (f32[2,256,256]{2,1,0:T(8,128)S(1)}, f32[2,256,256]{2,1,0:T(8,128)}, u32[]{:S(2)}) copy-start(f32[2,256,256]{2,1,0:T(8,128)} %wb.1) | copy-start | bytes 1572868
  1.7 2.2 %copy-start.1 = (f32[2,256,256]{2,1,0:T(8,128)S(1)}, f32[2,256,256]{2,1,0:T(8,128)}, u32[]{:S(2)}) copy-start(f32[2,256,256]{2,1,0:T(8,128)} %nb.1) | copy-start | bytes 1572868
